TPU v7x, 128 devices: a whole 4x4x4 slice. The times are simulated.
128 devices in a mesh: ep: 16 (over z, y), fsdp: 8 (over x, core).
Axes of the slice: x: 4, y: 4, z: 4, core: 2. Of those that a mesh axis runs over, the one named last changes fastest.
Arguments:
- tokens: bfloat16 [2048, 7168], P('ep'), may hold values from -6 to 6
- w_gate: bfloat16 [16, 7168, 2048], P('ep', None, 'fsdp'), may hold values from -0.0625 to 0.0625
- w_up: bfloat16 [16, 7168, 2048], P('ep', None, 'fsdp'), may hold values from -0.0625 to 0.0625
- tangent_down: bfloat16 [16, 2048, 7168], P('ep', 'fsdp'), may hold values from -0.1875 to 0.1875
- gates: float32 [2048, 2], P('ep'), may hold values from 0.1 to 1
- expert_ids: int32 [2048, 2], P('ep'), may hold values from 0 to 15, all different within a row; in each aligned block of 128 rows (0 to 127, 128 to 255, ...) at most 32 rows name the same one
Outputs:
- gn_product: float32 [16, 2048, 7168], P('ep', 'fsdp')
- tangent: bfloat16 [2048, 7168], P('ep', 'fsdp')
Inputs may be any that keep to these rules, and one draw needn't show every extreme that they name: `expert_ids`: each row names 2 different experts. Within the rows of one index of ep (128 tokens) no expert is named by more than 32 routes, a bound that some block reaches.
All inputs are finite; a program needn't handle non-finite values.
Results may differ from a plain program's by a relative error of at most 0.022.
Values may be sent and summed in bfloat16 or wider, within the bound.
A program may use at most 128 MiB of HBM per device.

v0:
```python
import jax
import jax.numpy as jnp
from jax import lax
from jax.sharding import PartitionSpec as P


def on_device(tokens, w_gate, w_up, tangent_down, gates, expert_ids):
    experts = lax.axis_size("ep")
    tok_rows, width = tokens.shape
    topk = expert_ids.shape[1]
    capacity = 2 * tok_rows * topk // experts
    routes = tok_rows * topk
    flat_ids = expert_ids.reshape(-1)
    onehot = (flat_ids[:, None] == jnp.arange(experts, dtype=jnp.int32)[None, :]).astype(jnp.int32)
    before = jnp.cumsum(onehot, axis=0) - onehot
    slot = jnp.sum(before * onehot, axis=1)
    dest = flat_ids * capacity + slot
    route_token = jnp.arange(routes, dtype=jnp.int32) // topk
    slot_token = jnp.full((experts * capacity,), tok_rows, jnp.int32).at[dest].set(route_token)
    slot_gate = jnp.zeros((experts * capacity,), jnp.float32).at[dest].set(gates.reshape(-1))
    outgoing = jnp.take(tokens, slot_token, axis=0, mode="fill", fill_value=0).reshape(
        experts, capacity, width
    )
    arrived, arrived_gate = (
        lax.all_to_all(outgoing, "ep", split_axis=0, concat_axis=0, tiled=True),
        lax.all_to_all(
            slot_gate.reshape(experts, capacity).astype(jnp.bfloat16),
            "ep",
            split_axis=0,
            concat_axis=0,
            tiled=True,
        ).astype(jnp.float32),
    )
    flat_rows = arrived.reshape(experts * capacity, width)
    first = jnp.dot(flat_rows, w_gate[0], preferred_element_type=jnp.float32)
    second = jnp.dot(flat_rows, w_up[0], preferred_element_type=jnp.float32)
    hidden = (jax.nn.silu(first) * second).astype(jnp.bfloat16)
    partial_value = jnp.dot(
        hidden, tangent_down[0], preferred_element_type=jnp.float32
    ) * arrived_gate.reshape(-1, 1)
    returned = lax.all_to_all(
        partial_value.reshape(experts, capacity, width).astype(jnp.bfloat16),
        "ep",
        split_axis=0,
        concat_axis=0,
        tiled=True,
    ).astype(jnp.float32)
    combined = (
        returned.reshape(experts * capacity, width)[dest].reshape(tok_rows, topk, width).sum(axis=1)
    )
    tangent_sum = lax.psum_scatter(
        combined.astype(jnp.bfloat16), "fsdp", scatter_dimension=1, tiled=True
    )
    whole = lax.all_gather(tangent_sum, "fsdp", axis=1, tiled=True)
    picked = jnp.take(whole, slot_token, axis=0, mode="fill", fill_value=0).astype(jnp.float32)
    weighted = (picked * slot_gate[:, None]).astype(jnp.bfloat16).reshape(experts, capacity, width)
    incoming = lax.all_to_all(weighted, "ep", split_axis=0, concat_axis=0, tiled=True)
    gn_local = lax.dot_general(
        hidden,
        incoming.reshape(experts * capacity, width),
        (((0,), (0,)), ((), ())),
        preferred_element_type=jnp.float32,
    )
    return (gn_local[None], tangent_sum)


def solution(mesh):
    in_specs = (
        P("ep", None),
        P("ep", None, "fsdp"),
        P("ep", None, "fsdp"),
        P("ep", "fsdp", None),
        P("ep", None),
        P("ep", None),
    )
    out_specs = (P("ep", "fsdp", None), P("ep", "fsdp"))
    return jax.shard_map(
        on_device, mesh=mesh, in_specs=in_specs, out_specs=out_specs, check_vma=False
    )
```

profile of v0, /device:TPU:1, one launch (start us, length us, event | category | flops | bytes accessed | tf_op | source)
XLA Modules:
  0.0 511.0 jit_solution(5157783738854764865)
XLA Ops:
  7.2 0.8 broadcast_multiply_fusion
  8.0 0.8 copy.14
  9.3 0.6 reduce-window.6
  9.9 0.2 slice_reduce_fusion
  10.2 0.8 copy.17
  11.2 1.4 scatter_custom_fusion.1
  12.6 0.7 convert_element_type.62
  13.3 8.6 %all-to-all-start.1 = ((bf16[16,1,32]{2,1,0:T(2,128)(2,1)}), bf16[16,1,32]{2,1,0:T(2,128)(2,1)S(1)}, u32[]{:S(2)}, u32[]{:S(2)}) async-start(bf16[16,1,32]{2,1,0:T(2,128)(2,1)} %convert_element_type.62), calls=%async_computation.1 | async-start | bytes 16384 | tf_op jit(solution)/shard_map/all_to_all | solution.py:26
  21.9 1.4 scatter_custom_fusion
  23.4 7.1 %gather_fusion.1 = bf16[512,7168]{1,0:T(8,128)(2,1)} fusion(bf16[128,7168]{1,0:T(8,128)(2,1)S(1)} %copy-done, s32[1024]{0:T(1024)S(1)} %pad_clamp_fusion.1), kind=kCustom, calls=%fused_computation.clone | custom fusion | bytes 14682112 | tf_op jit(solution)/shard_map/jit(_take)/gather | solution.py:21
  30.4 6.7 %broadcast_select_fusion = bf16[512,7168]{1,0:T(8,128)(2,1)} fusion(bf16[512,7168]{1,0:T(8,128)(2,1)} %gather_fusion.1, pred[512]{0:T(512)(128)(4,1)S(1)} %compare_and_fusion), kind=kLoop, calls=%fused_computation.9 | loop fusion | flops 3670016 | bytes 14680576 | tf_op jit(solution)/shard_map/jit(_take)/select_n | solution.py:21
  37.1 6.7 %all-to-all-start = ((bf16[16,32,7168]{2,1,0:T(8,128)(2,1)}), bf16[16,32,7168]{2,1,0:T(8,128)(2,1)}, u32[]{:S(2)}, u32[]{:S(2)}) async-start(bf16[16,32,7168]{2,1,0:T(8,128)(2,1)} %bitcast.54), calls=%async_computation | async-start | bytes 14680064 | tf_op jit(solution)/shard_map/all_to_all | solution.py:25
  43.9 106.5 %all-to-all-done = bf16[16,32,7168]{2,1,0:T(8,128)(2,1)} async-done(((bf16[16,32,7168]{2,1,0:T(8,128)(2,1)}), bf16[16,32,7168]{2,1,0:T(8,128)(2,1)}, u32[]{:S(2)}, u32[]{:S(2)}) %all-to-all-start) | async-done | bytes 7340064 | tf_op jit(solution)/shard_map/all_to_all | solution.py:25
  150.4 6.3 %fusion.3 = f32[512,256]{1,0:T(8,128)S(1)} fusion(bf16[512,7168]{1,0:T(8,128)(2,1)} %bitcast.4, bf16[1,7168,256]{2,1,0:T(8,128)(2,1)} %param.9), kind=kOutput, calls=%fused_computation.13 | convolution fusion | flops 1879048192 | bytes 11534336 | tf_op jit(solution)/shard_map/dot_general | solution.py:35
  156.8 5.3 %fusion.8 = bf16[512,256]{1,0:T(8,128)(2,1)S(1)} fusion(bf16[512,7168]{1,0:T(8,128)(2,1)} %bitcast.4, bf16[1,7168,256]{2,1,0:T(8,128)(2,1)S(1)} %copy-done.3, f32[512,256]{1,0:T(8,128)S(1)} %fusion.3), kind=kOutput, calls=%fused_computation.16 | convolution fusion | flops 1879834624 | bytes 11796480 | tf_op jit(solution)/shard_map/dot_general | solution.py:36
  162.1 5.2 %multiply_convert_fusion.1 = bf16[512,7168]{1,0:T(8,128)(2,1)} fusion(bf16[512,256]{1,0:T(8,128)(2,1)S(1)} %fusion.8, f32[512]{0:T(512)S(1)} %reshape.113, bf16[1,256,7168]{2,1,0:T(8,128)(2,1)S(1)} %copy-done.2), kind=kOutput, calls=%fused_computation.6 | convolution fusion | flops 1886388224 | bytes 11274240 | tf_op jit(solution)/shard_map/dot_general | solution.py:38
  167.3 5.2 %all-to-all-start.2 = ((bf16[16,32,7168]{2,1,0:T(8,128)(2,1)}), bf16[16,32,7168]{2,1,0:T(8,128)(2,1)}, u32[]{:S(2)}, u32[]{:S(2)}) async-start(bf16[16,32,7168]{2,1,0:T(8,128)(2,1)} %bitcast.56), calls=%async_computation.2 | async-start | bytes 14680064 | tf_op jit(solution)/shard_map/all_to_all | solution.py:41
  172.5 0.2 reduce-scatter.4.cloned.1.call-start
  172.8 104.2 %all-to-all-done.2 = bf16[16,32,7168]{2,1,0:T(8,128)(2,1)} async-done(((bf16[16,32,7168]{2,1,0:T(8,128)(2,1)}), bf16[16,32,7168]{2,1,0:T(8,128)(2,1)}, u32[]{:S(2)}, u32[]{:S(2)}) %all-to-all-start.2) | async-done | bytes 7340064 | tf_op jit(solution)/shard_map/all_to_all | solution.py:41
  277.0 10.2 %bitcast_convert_fusion = f32[512,7168]{1,0:T(8,128)} fusion(bf16[16,32,7168]{2,1,0:T(8,128)(2,1)} %all-to-all-done.2), kind=kLoop, calls=%fused_computation.8 | loop fusion | flops 3670016 | bytes 22020096 | tf_op jit(solution)/shard_map/reshape | solution.py:49
  287.2 14.1 %gather_fusion = f32[256,7168]{1,0:T(8,128)} fusion(f32[512,7168]{1,0:T(8,128)} %bitcast_convert_fusion, s32[1024]{0:T(1024)S(1)} %pad_clamp_fusion), kind=kCustom, calls=%fused_computation.2 | custom fusion | bytes 14681088 | tf_op jit(solution)/shard_map/gather | solution.py:49
  301.3 9.3 %reshape.110 = f32[128,2,7168]{2,1,0:T(2,128)} reshape(f32[256,7168]{1,0:T(8,128)} %gather_fusion) | data formatting | bytes 14680064 | tf_op jit(solution)/shard_map/reshape | solution.py:49
  310.5 10.7 %reduce_sum.22 = bf16[128,7168]{1,0:T(8,128)(2,1)S(1)} reduce(f32[128,2,7168]{2,1,0:T(2,128)} %reshape.110, f32[]{:T(128)} %constant.43.clone.1), dimensions={1}, to_apply=%region_5.7 | reduce | flops 917504 | bytes 9175044 | tf_op jit(solution)/shard_map/reduce_sum | solution.py:49
  321.2 2.3 copy.19
  323.5 0.3 all-gather.2.cloned.1.call-start
  323.8 32.4 %reduce-scatter.4.cloned.1.call-done = bf16[896,128]{1,0:T(8,128)(2,1)} async-done(((bf16[7168,128]{1,0:T(8,128)(2,1)}), bf16[896,128]{1,0:T(8,128)(2,1)}) %reduce-scatter.4.cloned.1.call-update) | async-done | bytes 229392
  356.2 1.8 copy.20
  358.0 27.7 %all-gather.2.cloned.1.call-done = bf16[128,7168]{1,0:T(8,128)(2,1)} async-done(((bf16[128,896]{1,0:T(8,128)(2,1)}), bf16[128,7168]{1,0:T(8,128)(2,1)}) %all-gather.2.cloned.1.call-update) | async-done | bytes 1835024 | tf_op jit(solution)/shard_map/all_gather | solution.py:54
  385.7 15.5 %gather_fusion.2 = bf16[512,7168]{1,0:T(8,128)(2,1)} fusion(bf16[128,7168]{1,0:T(8,128)(2,1)} %all-gather.2.cloned.1.call-done, s32[1024]{0:T(1024)S(1)} %pad_clamp_fusion.1), kind=kCustom, calls=%fused_computation.1.clone | custom fusion | bytes 14682112 | tf_op jit(solution)/shard_map/jit(_take)/gather | solution.py:55
  401.2 7.4 %multiply_convert_fusion = bf16[512,7168]{1,0:T(8,128)(2,1)S(1)} fusion(bf16[512,7168]{1,0:T(8,128)(2,1)} %gather_fusion.2, f32[512]{0:T(512)S(1)} %scatter_custom_fusion.1, pred[512]{0:T(512)(128)(4,1)S(1)} %compare_and_fusion), kind=kLoop, calls=%fused_computation.5 | loop fusion | flops 14680064 | bytes 14682624 | tf_op jit(solution)/shard_map/convert_element_type | solution.py:56
  408.6 90.4 %all_to_all.21 = bf16[16,32,7168]{2,1,0:T(8,128)(2,1)S(1)} all-to-all(bf16[16,32,7168]{2,1,0:T(8,128)(2,1)S(1)} %bitcast.55), channel_id=1, replica_groups=mesh['ep'=16,'fsdp'=8] {'ep'}, dimensions={0} | all-to-all | bytes 14680064 | tf_op jit(solution)/shard_map/all_to_all | solution.py:57
  499.0 5.2 %convolution_bitcast_fusion = f32[1,256,7168]{2,1,0:T(8,128)} fusion(bf16[512,256]{1,0:T(8,128)(2,1)S(1)} %fusion.8, bf16[512,7168]{1,0:T(8,128)(2,1)S(1)} %bitcast.53), kind=kOutput, calls=%fused_computation.7 | convolution fusion | flops 1879048192 | bytes 14942208 | tf_op jit(solution)/shard_map/dot_general | solution.py:58
  (29 shorter events, 1.0 us)
Async XLA Ops:
  7.2 16.2 %copy-start = (bf16[128,7168]{1,0:T(8,128)(2,1)S(1)}, bf16[128,7168]{1,0:T(8,128)(2,1)}, u32[]{:S(2)}) copy-start(bf16[128,7168]{1,0:T(8,128)(2,1)} %param.8) | copy-start | bytes 5505028
  13.3 23.8 %all-to-all-start.1 = ((bf16[16,1,32]{2,1,0:T(2,128)(2,1)}), bf16[16,1,32]{2,1,0:T(2,128)(2,1)S(1)}, u32[]{:S(2)}, u32[]{:S(2)}) async-start(bf16[16,1,32]{2,1,0:T(2,128)(2,1)} %convert_element_type.62), calls=%async_computation.1 | async-start | bytes 16384 | tf_op jit(solution)/shard_map/all_to_all | solution.py:26
  37.1 113.3 %all-to-all-start = ((bf16[16,32,7168]{2,1,0:T(8,128)(2,1)}), bf16[16,32,7168]{2,1,0:T(8,128)(2,1)}, u32[]{:S(2)}, u32[]{:S(2)}) async-start(bf16[16,32,7168]{2,1,0:T(8,128)(2,1)} %bitcast.54), calls=%async_computation | async-start | bytes 14680064 | tf_op jit(solution)/shard_map/all_to_all | solution.py:25
  150.4 6.3 %copy-start.3 = (bf16[1,7168,256]{2,1,0:T(8,128)(2,1)S(1)}, bf16[1,7168,256]{2,1,0:T(8,128)(2,1)}, u32[]{:S(2)}) copy-start(bf16[1,7168,256]{2,1,0:T(8,128)(2,1)} %param.10) | copy-start | bytes 11010052
  156.8 5.3 %copy-start.2 = (bf16[1,256,7168]{2,1,0:T(8,128)(2,1)S(1)}, bf16[1,256,7168]{2,1,0:T(8,128)(2,1)}, u32[]{:S(2)}) copy-start(bf16[1,256,7168]{2,1,0:T(8,128)(2,1)} %param.11) | copy-start | bytes 11010052
  167.3 109.7 %all-to-all-start.2 = ((bf16[16,32,7168]{2,1,0:T(8,128)(2,1)}), bf16[16,32,7168]{2,1,0:T(8,128)(2,1)}, u32[]{:S(2)}, u32[]{:S(2)}) async-start(bf16[16,32,7168]{2,1,0:T(8,128)(2,1)} %bitcast.56), calls=%async_computation.2 | async-start | bytes 14680064 | tf_op jit(solution)/shard_map/all_to_all | solution.py:41
  172.5 183.6 %reduce-scatter.4.cloned.1.call-start = ((), (), s32[]{:S(2)}) async-start(), calls=%async_computation.6 | async-start | bytes 2064384
  323.5 62.2 %all-gather.2.cloned.1.call-start = ((), (), s32[]{:S(2)}) async-start(), calls=%async_computation.5 | async-start | bytes 2064384 | tf_op jit(solution)/shard_map/all_gather | solution.py:54
  499.0 5.2 %copy-start.1 = (bf16[128,7168]{1,0:T(8,128)(2,1)S(1)}, bf16[128,7168]{1,0:T(8,128)(2,1)}, u32[]{:S(2)}) copy-start(bf16[128,7168]{1,0:T(8,128)(2,1)} %param.8) | copy-start | bytes 5505028
Sparse Core Ops, SparseCore 0:
  323.6 32.4 reduce-scatter.3
  358.4 27.1 all-gather.1
where the time goes:
time: 512 us; the launch traced here: 511 us
  waiting for transfers between devices  271 us (53%)
  blocking collectives  90.4 us (18%)
  local copies, waits for them, and re-layouts  56 us (11%)
  other arithmetic  36.6 us (7%)
  matrix products  22 us (4%)
  starting transfers between devices  21 us (4%)
  between operations  14.2 us (3%)
    all_to_all x1, waiting for transfers between devices, on_device(): lax.all_to_all(outgoing, 'ep', split_axis=0, concat_axis=0, tiled=True)  107 us
    all_to_all x1, waiting for transfers between devices, on_device(): lax.all_to_all(partial_value.reshape(experts, capacity, width).astype(jnp...  104 us
    all_to_all x1, blocking collectives, on_device(): lax.all_to_all(weighted, 'ep', split_axis=0, concat_axis=0, tiled=True)  90.4 us
    unnamed x3, waiting for transfers between devices  32.4 us
    all_gather x1, waiting for transfers between devices, on_device(): whole = lax.all_gather(tangent_sum, 'fsdp', axis=1, tiled=True)  27.7 us
    gather x1, local copies, waits for them, and re-layouts, on_device(): jnp.take(whole, slot_token, axis=0, mode='fill', fill_value=0)  15.5 us
    gather x1, local copies, waits for them, and re-layouts, on_device(): returned.reshape(experts * capacity, width)[dest]  14.1 us
    reduce_sum x1, other arithmetic, on_device(): returned.reshape(experts * capacity, width)[dest]  10.7 us
  transfers between devices with their start and end apart: 5, of which 4 were waited for; matrix products, arithmetic and copies ran while one was open for 3% of the time, Pallas kernels for 0%

commit v1 on v0

v1 whole, which is shorter than its diff:
```python
import functools

import jax
import jax.numpy as jnp
from jax import lax
from jax.experimental import pallas as pl
from jax.experimental.pallas import tpu as pltpu
from jax.sharding import PartitionSpec as P

MESH = pl.DeviceIdType.MESH
F32 = jnp.float32
BF16 = jnp.bfloat16


def spans(widths):
    out, at = [], 0
    for w in widths:
        out.append((at, w))
        at += w
    return out


def dot(a, b):
    return jnp.dot(a, b, preferred_element_type=F32)


class Place:
    def __init__(self):
        self.e = lax.axis_index("ep")
        self.f = lax.axis_index("fsdp")
        self.x = self.f // 2
        self.c = self.f - 2 * self.x
        self.pair = 2 * self.x + 1 - self.c

    def chip(self, off):
        return lax.rem(self.x + off, 4)

    def chunk(self, off, other=False):
        return 2 * self.chip(off) + (1 - self.c if other else self.c)

    def right(self):
        return (self.e, self.chunk(1))

    def left(self):
        return (self.e, self.chunk(3))

    def other(self):
        return (self.e, self.pair)


class AllToAll:
    def __init__(self, at, experts, cap, src, dst, send, recv, pieces):
        self.__dict__.update(locals())

    def start(self, p):
        at, cap = self.at, self.cap
        a, w = self.pieces[p]

        def one(d, carry):
            to = lax.rem(at.e + d, self.experts)
            pltpu.make_async_remote_copy(
                src_ref=self.src.at[pl.ds(pl.multiple_of(to * cap, cap), cap), pl.ds(a, w)],
                dst_ref=self.dst.at[pl.ds(pl.multiple_of(at.e * cap, cap), cap), pl.ds(a, w)],
                send_sem=self.send.at[p],
                recv_sem=self.recv.at[p],
                device_id=(to, at.f),
                device_id_type=MESH,
            ).start()
            return carry

        lax.fori_loop(1, self.experts, one, 0)

    def _all(self, p, sem):
        a, w = self.pieces[p]
        ref = self.src.at[pl.ds(0, (self.experts - 1) * self.cap), pl.ds(a, w)]
        pltpu.make_async_copy(ref, ref, sem.at[p]).wait()

    def wait(self, p):
        self._all(p, self.recv)

    def drain(self, p):
        self._all(p, self.send)


class Gather:
    KINDS = 8

    def __init__(self, at, buf, send, recv, pieces):
        self.__dict__.update(locals())
        self.rows = buf.shape[1]

    def copy(self, p, kind):
        at, half = self.at, self.rows // 2
        a, w = self.pieces[p]
        off = (0, 0, 0, 3, 1, 3, 1, 2)[kind]
        to = (at.other, at.right, at.left, at.right, at.left, at.other, at.other, at.other)[kind]()
        r0, n = {3: (0, half), 4: (half, half)}.get(kind, (0, self.rows))
        ref = self.buf.at[at.chunk(off), pl.ds(r0, n), pl.ds(a, w)]
        return pltpu.make_async_remote_copy(
            src_ref=ref,
            dst_ref=ref,
            send_sem=self.send.at[p, kind],
            recv_sem=self.recv.at[p, kind],
            device_id=to,
            device_id_type=MESH,
        )

    def one(self, p):
        for kind in (1, 2, 0):
            self.copy(p, kind).start()

    def two(self, p):
        self.copy(p, 1).wait_recv()
        self.copy(p, 3).start()
        self.copy(p, 2).wait_recv()
        self.copy(p, 4).start()
        self.copy(p, 5).start()
        self.copy(p, 6).start()

    def three(self, p):
        self.copy(p, 3).wait_recv()
        self.copy(p, 4).wait_recv()
        self.copy(p, 7).start()

    def done(self, p):
        for kind in (0, 5, 6, 7):
            self.copy(p, kind).wait_recv()

    def drain(self, p):
        for kind in range(self.KINDS):
            self.copy(p, kind).wait_send()


def kernel(
    pieces, experts, cap,
    ids_ref, gates_ref, tok_ref, wg_ref, wu_ref, td_ref,
    gn_ref, tan_ref,
    tokv, wgv, wuv, tdv, sel, gsl, comb_hi, comb_lo, send, xbuf, acc_g, acc_u, hid, hid_t,
    psend, precv, rsend, rrecv, fin, ret, wsend, wbuf, gnv,
    load, a_sem, g_send, g_recv, r_send, r_recv, out_sem,
):
    at = Place()
    n = len(pieces)
    toks, chunk = tokv.shape
    rows = experts * cap
    half = rows // 2

    loads = [pltpu.make_async_copy(
        tok_ref.at[:, pl.ds(pl.multiple_of(at.f * chunk, 128), chunk)], tokv, load.at[0])]
    loads += [pltpu.make_async_copy(wg_ref.at[0], wgv, load.at[1]),
              pltpu.make_async_copy(wu_ref.at[0], wuv, load.at[2])]
    loads += [pltpu.make_async_copy(
        td_ref.at[0, :, pl.ds(k * chunk, chunk)], tdv.at[k], load.at[3 + k]) for k in range(8)]
    for copy in loads:
        copy.start()

    barrier = pltpu.get_barrier_semaphore()

    def greet(d, carry):
        pl.semaphore_signal(
            barrier, inc=1, device_id=(lax.rem(at.e + d, experts), at.f), device_id_type=MESH)
        return carry

    lax.fori_loop(1, experts, greet, 0)
    for to in (at.right(), at.left(), at.other()):
        pl.semaphore_signal(barrier, inc=1, device_id=to, device_id_type=MESH)

    lane = lax.broadcasted_iota(jnp.int32, (toks, 128), 1)
    named = [ids_ref[:, k:k + 1] == lane for k in range(ids_ref.shape[1])]
    mask = sum(jnp.where(m, 1.0, 0.0) for m in named)
    gate = sum(jnp.where(m, gates_ref[:, k:k + 1], 0.0) for k, m in enumerate(named))
    mask_t, gate_t = mask.T, gate.T
    earlier = jnp.where(
        lax.broadcasted_iota(jnp.int32, (toks, toks), 0)
        < lax.broadcasted_iota(jnp.int32, (toks, toks), 1), 1.0, 0.0)
    rank_t = dot(mask_t.astype(BF16), earlier.astype(BF16))
    place = lax.broadcasted_iota(jnp.int32, (cap, toks), 0).astype(F32)
    for k in range(experts):
        here = (rank_t[k:k + 1, :] == place) & (mask_t[k:k + 1, :] > 0.5)
        picked = jnp.where(here, gate_t[k:k + 1, :], 0.0)
        sel[k * cap:(k + 1) * cap, :] = jnp.where(here, 1.0, 0.0).astype(BF16)
        gsl[k * cap:(k + 1) * cap, :] = jnp.sum(picked, axis=1, keepdims=True)
        picked_t = picked.T
        hi = picked_t.astype(BF16)
        comb_hi[k] = hi
        comb_lo[k] = (picked_t - hi.astype(F32)).astype(BF16)

    mine = pl.ds(pl.multiple_of(at.e * cap, cap), cap)
    loads[0].wait()
    for a, w in pieces:
        send[:, a:a + w] = dot(sel[...], tokv[:, a:a + w]).astype(BF16)
        xbuf[at.f, mine, a:a + w] = send[mine, a:a + w]
    acc_g[...] = jnp.zeros_like(acc_g)
    acc_u[...] = jnp.zeros_like(acc_u)

    pl.semaphore_wait(barrier, experts - 1 + 3)

    out_a = AllToAll(at, experts, cap, send, xbuf.at[at.f], a_sem.at[0], a_sem.at[1], pieces)
    out_g = Gather(at, xbuf, g_send.at[0], g_recv.at[0], pieces)

    def up(p):
        a, w = pieces[p]

        def tile(m, carry):
            r = pl.ds(pl.multiple_of(m * half, half), half)
            g, u = acc_g[r, :], acc_u[r, :]
            for k in range(8):
                xk = xbuf[k, r, a:a + w]
                g += dot(xk, wgv[k * chunk + a:k * chunk + a + w, :])
                u += dot(xk, wuv[k * chunk + a:k * chunk + a + w, :])
            acc_g[r, :] = g
            acc_u[r, :] = u
            return carry

        lax.fori_loop(0, 2, tile, 0)

    def in_steps(stages):
        for t in range(n + len(stages) - 1):
            for s, stage in enumerate(stages):
                if 0 <= t - s < n:
                    stage(t - s)

    for p in range(n):
        out_a.start(p)

    def x_one(p):
        out_a.wait(p)
        out_g.one(p)

    def x_up(p):
        if p == 0:
            loads[1].wait()
            loads[2].wait()
        out_g.done(p)
        up(p)

    in_steps([x_one, out_g.two, out_g.three, x_up])

    def silu(m, carry):
        r = pl.ds(pl.multiple_of(m * cap, cap), cap)
        g = acc_g[r, :]
        hid[r, :] = (g / (1.0 + jnp.exp(-g)) * acc_u[r, :]).astype(BF16)
        return carry

    lax.fori_loop(0, rows // cap, silu, 0)
    hid_t[...] = hid[...].astype(F32).T.astype(BF16)
    for copy in loads[3:]:
        copy.wait()

    offs = (2, 1, 3, 0)

    def rcopy(p, kind):
        a, w = pieces[p]
        cols = pl.ds(a, w)
        whole, top, low = pl.ds(0, rows), pl.ds(0, half), pl.ds(half, half)
        if kind < 4:
            src, dst, r, to = psend.at[kind], precv.at[kind], whole, at.other()
        else:
            src, dst, r, to = (
                (rsend.at[0], rrecv.at[0], top, at.right()),
                (rsend.at[0], rrecv.at[0], low, at.left()),
                (rsend.at[1], rrecv.at[1], whole, at.right()),
                (rsend.at[2], rrecv.at[2], whole, at.left()),
            )[kind - 4]
        return pltpu.make_async_remote_copy(
            src_ref=src.at[r, cols], dst_ref=dst.at[r, cols],
            send_sem=r_send.at[p, kind], recv_sem=r_recv.at[p, kind],
            device_id=to, device_id_type=MESH)

    def partial(p, j, other, m):
        a, w = pieces[p]
        r = pl.ds(pl.multiple_of(m * half, half), half)
        return r, dot(hid[r, :], tdv[at.chunk(offs[j], other), :, a:a + w])

    def to_pair(p):
        a, w = pieces[p]
        for j in range(4):
            def tile(m, carry):
                r, v = partial(p, j, True, m)
                psend[j, r, a:a + w] = v.astype(BF16)
                return carry

            lax.fori_loop(0, 2, tile, 0)
            rcopy(p, j).start()

    def summed(p, j, m, adds):
        a, w = pieces[p]
        r, v = partial(p, j, False, m)
        v += precv[j, r, a:a + w].astype(F32)
        for k in adds:
            v += rrecv[k, r, a:a + w].astype(F32)
        return r, v.astype(BF16)

    def far(p):
        a, w = pieces[p]
        rcopy(p, 0).wait_recv()
        for m in range(2):
            r, v = summed(p, 0, m, ())
            rsend[0, r, a:a + w] = v
            rcopy(p, 4 + m).start()

    def near(p):
        a, w = pieces[p]
        for j in (1, 2):
            rcopy(p, j).wait_recv()
            rcopy(p, 3 + j).wait_recv()
            for m in range(2):
                r, v = summed(p, j, m, (0,) if m == j - 1 else ())
                rsend[j, r, a:a + w] = v
            rcopy(p, 5 + j).start()

    back = AllToAll(at, experts, cap, fin, ret, a_sem.at[2], a_sem.at[3], pieces)

    def home(p):
        a, w = pieces[p]
        for kind in (3, 6, 7):
            rcopy(p, kind).wait_recv()
        for m in range(2):
            r, v = summed(p, 3, m, (1, 2))
            fin[r, a:a + w] = v
        back.start(p)
        ret[mine, a:a + w] = fin[mine, a:a + w]

    out_w = AllToAll(at, experts, cap, wsend, wbuf.at[at.f], a_sem.at[4], a_sem.at[5], pieces)
    out_v = Gather(at, wbuf, g_send.at[1], g_recv.at[1], pieces)

    def combine(p):
        a, w = pieces[p]
        back.wait(p)
        total = jnp.zeros((toks, w), F32)
        for k in range(experts):
            got = ret[k * cap:(k + 1) * cap, a:a + w]
            total += dot(comb_hi[k], got) + dot(comb_lo[k], got)
        tangent = total.astype(BF16)
        tan_ref[:, a:a + w] = tangent
        for m in range(2):
            r = pl.ds(m * half, half)
            wsend[r, a:a + w] = (dot(sel[r, :], tangent) * gsl[r, :]).astype(BF16)
        out_w.start(p)
        wbuf[at.f, mine, a:a + w] = wsend[mine, a:a + w]

    def w_one(p):
        out_w.wait(p)
        out_v.one(p)

    def out_copy(p, k):
        a, w = pieces[p]
        return pltpu.make_async_copy(
            gnv.at[k, :, pl.ds(a, w)], gn_ref.at[0, :, pl.ds(k * chunk + a, w)], out_sem.at[p, k])

    def product(p):
        a, w = pieces[p]
        out_v.done(p)
        for k in range(8):
            gnv[k, :, a:a + w] = dot(hid_t[...], wbuf[k, :, a:a + w])
            out_copy(p, k).start()

    in_steps([to_pair, far, near, home, combine, w_one, out_v.two, out_v.three, product])

    for p in range(n):
        for moved in (out_a, back, out_w, out_g, out_v):
            moved.drain(p)
        for kind in range(8):
            rcopy(p, kind).wait_send()
        for k in range(8):
            out_copy(p, k).wait()


def on_device(widths, cap, tokens, w_gate, w_up, tangent_down, gates, expert_ids):
    experts = lax.axis_size("ep")
    toks, width = tokens.shape
    chunk = width // 8
    hidden = w_gate.shape[2]
    rows = experts * cap
    pieces = spans(widths)
    n = len(pieces)
    vmem, anywhere = pl.BlockSpec(memory_space=pltpu.VMEM), pl.BlockSpec(memory_space=pl.ANY)
    gn, tangent = pl.pallas_call(
        functools.partial(kernel, pieces, experts, cap),
        out_shape=(
            jax.ShapeDtypeStruct((1, hidden, width), F32),
            jax.ShapeDtypeStruct((toks, chunk), BF16),
        ),
        in_specs=[vmem, vmem, anywhere, anywhere, anywhere, anywhere],
        out_specs=(anywhere, vmem),
        scratch_shapes=[
            pltpu.VMEM((toks, chunk), BF16),
            pltpu.VMEM((width, hidden), BF16),
            pltpu.VMEM((width, hidden), BF16),
            pltpu.VMEM((8, hidden, chunk), BF16),
            pltpu.VMEM((rows, toks), BF16),
            pltpu.VMEM((rows, 1), F32),
            pltpu.VMEM((experts, toks, cap), BF16),
            pltpu.VMEM((experts, toks, cap), BF16),
            pltpu.VMEM((rows, chunk), BF16),
            pltpu.VMEM((8, rows, chunk), BF16),
            pltpu.VMEM((rows, hidden), F32),
            pltpu.VMEM((rows, hidden), F32),
            pltpu.VMEM((rows, hidden), BF16),
            pltpu.VMEM((hidden, rows), BF16),
            pltpu.VMEM((4, rows, chunk), BF16),
            pltpu.VMEM((4, rows, chunk), BF16),
            pltpu.VMEM((3, rows, chunk), BF16),
            pltpu.VMEM((3, rows, chunk), BF16),
            pltpu.VMEM((rows, chunk), BF16),
            pltpu.VMEM((rows, chunk), BF16),
            pltpu.VMEM((rows, chunk), BF16),
            pltpu.VMEM((8, rows, chunk), BF16),
            pltpu.VMEM((8, hidden, chunk), F32),
            pltpu.SemaphoreType.DMA((11,)),
            pltpu.SemaphoreType.DMA((6, n)),
            pltpu.SemaphoreType.DMA((2, n, 8)),
            pltpu.SemaphoreType.DMA((2, n, 8)),
            pltpu.SemaphoreType.DMA((n, 8)),
            pltpu.SemaphoreType.DMA((n, 8)),
            pltpu.SemaphoreType.DMA((n, 8)),
        ],
        compiler_params=pltpu.CompilerParams(
            collective_id=0, has_side_effects=True, vmem_limit_bytes=60 * 2**20),
    )(expert_ids, gates, tokens, w_gate, w_up, tangent_down)
    return gn, tangent


def solution(mesh, widths=(256, 256, 384), cap=32):
    in_specs = (
        P("ep", None),
        P("ep", None, "fsdp"),
        P("ep", None, "fsdp"),
        P("ep", "fsdp", None),
        P("ep", None),
        P("ep", None),
    )
    out_specs = (P("ep", "fsdp", None), P("ep", "fsdp"))
    return jax.shard_map(
        functools.partial(on_device, widths, cap),
        mesh=mesh, in_specs=in_specs, out_specs=out_specs, check_vma=False,
    )
```

time: 512 us -> 140 us (0.27)
  waiting for transfers between devices: 271 us -> 0 us
  Pallas kernels: 0 us -> 129 us
  blocking collectives: 90.4 us -> 0 us
  local copies, waits for them, and re-layouts: 56 us -> 10.5 us
  other arithmetic: 36.6 us -> 0 us
  matrix products: 22 us -> 0 us
  starting transfers between devices: 21 us -> 0 us
  between operations: 14.2 us -> 0.65 us
    all_to_all x3 -> x0, waiting for transfers between devices: 211 us -> none  [the longest x1 107 us: on_device(): lax.all_to_all(outgoing, 'ep', split_axis=0, concat_axis=0, tiled=True)]
    pallas_call x0 -> x1, Pallas kernels: none -> 129 us  [on_device(): pl.pallas_call(functools.partial(kernel, pieces, experts, cap), out_shape...]
    all_to_all x1 -> x0, blocking collectives: 90.4 us -> none  [on_device(): lax.all_to_all(weighted, 'ep', split_axis=0, concat_axis=0, tiled=True)]
    gather x3 -> x0, local copies, waits for them, and re-layouts: 36.7 us -> none  [the longest x1 15.5 us: on_device(): jnp.take(whole, slot_token, axis=0, mode='fill', fill_value=0)]
    unnamed x3 -> x0, waiting for transfers between devices: 32.4 us -> none
    all_gather x1 -> x0, waiting for transfers between devices: 27.7 us -> none  [on_device(): whole = lax.all_gather(tangent_sum, 'fsdp', axis=1, tiled=True)]
    dot_general x4 -> x0, matrix products: 22 us -> none  [the longest x1 6.33 us: on_device(): first = jnp.dot(flat_rows, w_gate[0], preferred_element_type=jnp.float32)]
    all_to_all x3 -> x0, starting transfers between devices: 20.5 us -> none  [the longest x1 8.6 us: on_device(): lax.all_to_all(slot_gate.reshape(experts, capacity).astype(jnp.bfloat16),...]
  transfers between devices with their start and end apart: 5 -> 0, of which waited for: 4 -> 0; matrix products, arithmetic and copies ran while one was open for 3% -> 0% of each run, Pallas kernels for 0% -> 0%
where the time goes in v1:
time: 140 us
  Pallas kernels  129 us (92%)
  local copies, waits for them, and re-layouts  10.5 us (8%)
    pallas_call x1, Pallas kernels, on_device(): pl.pallas_call(functools.partial(kernel, pieces, experts, cap), out_shape...  129 us
    unnamed x6, local copies, waits for them, and re-layouts  10.5 us

profile of v1, /device:TPU:1, one launch (start us, length us, event | category | flops | bytes accessed | tf_op | source)
XLA Modules:
  0.0 140.1 jit_solution(1950141733104817548)
XLA Ops:
  0.6 1.4 %copy.9.gates_ref = f32[128,2]{1,0:T(8,128)} copy(f32[128,2]{0,1:T(2,128)} %param.10) | data formatting | bytes 2048 | tf_op args[4]
  2.0 1.4 %copy.8.ids_ref = s32[128,2]{1,0:T(8,128)} copy(s32[128,2]{0,1:T(2,128)} %param.11) | data formatting | bytes 2048 | tf_op args[5]
  3.5 129.0 %shard_map.77 = (f32[1,256,7168]{2,1,0:T(8,128)}, bf16[128,896]{1,0:T(8,128)(2,1)}) custom-call(s32[128,2]{1,0:T(8,128)} %copy.8.ids_ref, f32[128,2]{1,0:T(8,128)} %copy.9.gates_ref, bf16[128,7168]{1,0:T(8,128)(2,1)} %tok_ref.1, bf16[1,7168,256]{2,1,0:T(8,128)(2,1)} %wg_ref.1, bf16[1,7168,256]{2,1,0:T(8,128)(2,1)} %wu_ref.1, bf16[1,256,7168]{2,1,0:T(8,128)(2,1)} %td_ref.1), custom_call_target="tpu_custom_call" | custom-call | tf_op jit(solution)/shard_map/pallas_call | solution.py:378
  132.5 0.0 copy-start
  132.5 7.0 %copy.12 = f32[1,256,7168]{2,1,0:T(8,128)} copy(f32[1,256,7168]{2,1,0:T(8,128)} %get-tuple-element.4) | data formatting | bytes 14680064
  139.4 0.0 copy-done
  139.4 0.7 copy.13
Async XLA Ops:
  132.5 7.0 %copy-start = (bf16[128,896]{1,0:T(8,128)(2,1)S(1)}, bf16[128,896]{1,0:T(8,128)(2,1)}, u32[]{:S(2)}) copy-start(bf16[128,896]{1,0:T(8,128)(2,1)} %get-tuple-element.5) | copy-start | bytes 688132

commit v2 on v1

v2 whole, which is shorter than its diff:
```python
import functools

import jax
import jax.numpy as jnp
from jax import lax
from jax.experimental import pallas as pl
from jax.experimental.pallas import tpu as pltpu
from jax.sharding import PartitionSpec as P

MESH = pl.DeviceIdType.MESH
F32 = jnp.float32
BF16 = jnp.bfloat16


def spans(widths):
    out, at = [], 0
    for w in widths:
        out.append((at, w))
        at += w
    return out


def dot(a, b):
    return jnp.dot(a, b, preferred_element_type=F32)


def cbh(k):
    return k % 2, k // 2 % 2, k // 4


class Place:
    def __init__(self):
        self.e = lax.axis_index("ep")
        self.f = lax.axis_index("fsdp")
        self.x = self.f // 2
        self.c = self.f - 2 * self.x
        self.h = self.x // 2
        self.b = self.x - 2 * self.h

    def chip(self, off):
        return lax.rem(self.x + off, 4)

    def chunk(self, off, other=False):
        return 2 * self.chip(off) + (1 - self.c if other else self.c)

    def to(self, off):
        return (self.e, self.chunk(off))

    def pair(self):
        return (self.e, self.chunk(0, True))


class AllToAll:
    def __init__(self, at, experts, cap, src, dst, send, recv, pieces):
        self.__dict__.update(locals())

    def start(self, p):
        at, cap = self.at, self.cap
        a, w = self.pieces[p]

        def one(d, carry):
            to = lax.rem(at.e + d, self.experts)
            pltpu.make_async_remote_copy(
                src_ref=self.src.at[:, pl.ds(pl.multiple_of(to * cap, cap), cap), pl.ds(a, w)],
                dst_ref=self.dst.at[:, pl.ds(pl.multiple_of(at.e * cap, cap), cap), pl.ds(a, w)],
                send_sem=self.send.at[p],
                recv_sem=self.recv.at[p],
                device_id=(to, at.f),
                device_id_type=MESH,
            ).start()
            return carry

        lax.fori_loop(1, self.experts, one, 0)

    def _all(self, p, sem):
        a, w = self.pieces[p]
        ref = self.src.at[:, pl.ds(0, (self.experts - 1) * self.cap), pl.ds(a, w)]
        pltpu.make_async_copy(ref, ref, sem.at[p]).wait()

    def wait(self, p):
        self._all(p, self.recv)

    def drain(self, p):
        self._all(p, self.send)


class Gather:
    KINDS = 5

    def __init__(self, at, buf, send, recv, pieces):
        self.__dict__.update(locals())

    def copy(self, p, kind):
        at = self.at
        a, w = self.pieces[p]
        cols = pl.ds(a, w)
        if kind == 2:
            ref = self.buf.at[at.c, at.b, :, :, cols]
        elif kind < 2:
            ref = self.buf.at[at.c, at.b, at.h, :, cols]
        else:
            ref = self.buf.at[at.c, 1 - at.b, at.chip(3 if kind == 3 else 1) // 2, :, cols]
        to = (at.to(1), at.to(3), at.pair(), at.pair(), at.pair())[kind]
        return pltpu.make_async_remote_copy(
            src_ref=ref,
            dst_ref=ref,
            send_sem=self.send.at[p, kind],
            recv_sem=self.recv.at[p, kind],
            device_id=to,
            device_id_type=MESH,
        )

    def one(self, p):
        for kind in (0, 1, 2):
            self.copy(p, kind).start()

    def two(self, p):
        for kind in (0, 1):
            self.copy(p, kind).wait_recv()
            self.copy(p, kind + 3).start()

    def done(self, p):
        for kind in (2, 3, 4):
            self.copy(p, kind).wait_recv()

    def drain(self, p):
        for kind in range(self.KINDS):
            self.copy(p, kind).wait_send()


def kernel(
    xpieces, pieces, experts, cap, upto,
    ids_ref, gates_ref, tok_ref, wg_ref, wu_ref, td_ref,
    gn_ref, tan_ref,
    tokv, wgv, wuv, tdv, sel, selg, gsl, comb_hi, comb_lo, send, xbuf, acc_g, acc_u, hid, hid_t,
    psend, precv, rsend, rrecv, fin, ret, tsend, trecv, wsend, wbuf, gnv,
    load, x_sem, a_sem, xg_send, xg_recv, g_send, g_recv, r_send, r_recv, out_sem,
):
    at = Place()
    nx, n = len(xpieces), len(pieces)
    toks, chunk = tokv.shape[1:]
    rows = experts * cap
    half = rows // 2
    drains = []

    loads = [pltpu.make_async_copy(
        tok_ref.at[:, pl.ds(pl.multiple_of((4 * h + 2 * at.b + at.c) * chunk, 128), chunk)],
        tokv.at[h], load.at[h]) for h in range(2)]
    loads += [pltpu.make_async_copy(wg_ref.at[0], wgv, load.at[2]),
              pltpu.make_async_copy(wu_ref.at[0], wuv, load.at[3])]
    loads += [pltpu.make_async_copy(
        td_ref.at[0, :, pl.ds(k * chunk, chunk)], tdv.at[k], load.at[4 + k]) for k in range(8)]
    for copy in loads:
        copy.start()

    barrier = pltpu.get_barrier_semaphore()

    def greet(d, carry):
        pl.semaphore_signal(
            barrier, inc=1, device_id=(lax.rem(at.e + d, experts), at.f), device_id_type=MESH)
        return carry

    lax.fori_loop(1, experts, greet, 0)
    for to in (at.to(1), at.to(3), at.to(2), at.pair()):
        pl.semaphore_signal(barrier, inc=1, device_id=to, device_id_type=MESH)

    expert = lax.broadcasted_iota(jnp.int32, (experts, toks), 0)
    named = [ids_ref[k:k + 1, :] == expert for k in range(ids_ref.shape[0])]
    mask_t = sum(jnp.where(m, 1.0, 0.0) for m in named)
    gate_t = sum(jnp.where(m, gates_ref[k:k + 1, :], 0.0) for k, m in enumerate(named))
    earlier = jnp.where(
        lax.broadcasted_iota(jnp.int32, (toks, toks), 0)
        < lax.broadcasted_iota(jnp.int32, (toks, toks), 1), 1.0, 0.0)
    rank_t = dot(mask_t.astype(BF16), earlier.astype(BF16))
    place = lax.broadcasted_iota(jnp.int32, (cap, toks), 0).astype(F32)
    for k in range(experts):
        here = (rank_t[k:k + 1, :] == place) & (mask_t[k:k + 1, :] > 0.5)
        picked = jnp.where(here, gate_t[k:k + 1, :], 0.0)
        sel[k * cap:(k + 1) * cap, :] = jnp.where(here, 1.0, 0.0).astype(BF16)
        selg[k * cap:(k + 1) * cap, :] = picked
        gsl[k * cap:(k + 1) * cap, :] = jnp.sum(picked, axis=1, keepdims=True)

    mine = pl.ds(pl.multiple_of(at.e * cap, cap), cap)
    loads[0].wait()
    loads[1].wait()
    for a, w in xpieces:
        for h in range(2):
            send[h, :, a:a + w] = dot(sel[...], tokv[h, :, a:a + w]).astype(BF16)
            xbuf[at.c, at.b, h, mine, a:a + w] = send[h, mine, a:a + w]

    pl.semaphore_wait(barrier, experts - 1 + 4)

    out_a = AllToAll(
        at, experts, cap, send, xbuf.at[at.c, at.b], x_sem.at[0], x_sem.at[1], xpieces)
    out_g = Gather(at, xbuf, xg_send, xg_recv, xpieces)
    for p in range(nx):
        out_a.start(p)

    acc_g[...] = jnp.zeros_like(acc_g)
    acc_u[...] = jnp.zeros_like(acc_u)
    comb = selg[...].T
    hi = comb.astype(BF16)
    comb_hi[...] = hi
    comb_lo[...] = (comb - hi.astype(F32)).astype(BF16)

    def up(p):
        a, w = xpieces[p]

        def tile(m, carry):
            r = pl.ds(pl.multiple_of(m * half, half), half)
            g, u = acc_g[r, :], acc_u[r, :]
            for k in range(8):
                xk = xbuf[*cbh(k), r, a:a + w]
                g += dot(xk, wgv[k * chunk + a:k * chunk + a + w, :])
                u += dot(xk, wuv[k * chunk + a:k * chunk + a + w, :])
            acc_g[r, :] = g
            acc_u[r, :] = u
            return carry

        lax.fori_loop(0, 2, tile, 0)

    def in_steps(n, stages):
        for t in range(n + len(stages) - 1):
            for s, stage in enumerate(stages):
                if 0 <= t - s < n:
                    stage(t - s)

    def x_one(p):
        out_a.wait(p)
        out_g.one(p)

    def x_up(p):
        if p == 0:
            loads[2].wait()
            loads[3].wait()
        out_g.done(p)
        up(p)

    in_steps(nx, [x_one, out_g.two, x_up])
    drains += [(out_a.drain, nx), (out_g.drain, nx)]

    def silu(m, carry):
        r = pl.ds(pl.multiple_of(m * cap, cap), cap)
        g = acc_g[r, :]
        hid[r, :] = (g / (1.0 + jnp.exp(-g)) * acc_u[r, :]).astype(BF16)
        return carry

    lax.fori_loop(0, rows // cap, silu, 0)
    for copy in loads[4:]:
        copy.wait()

    offs = (1, 3, 2, 0)

    def rcopy(p, kind):
        a, w = pieces[p]
        if kind < 4:
            src, dst, to = psend.at[kind], precv.at[kind], at.pair()
        else:
            src, dst, to = rsend.at[kind - 4], rrecv.at[kind - 4], at.to(1 if kind == 4 else 3)
        return pltpu.make_async_remote_copy(
            src_ref=src.at[:, pl.ds(a, w)], dst_ref=dst.at[:, pl.ds(a, w)],
            send_sem=r_send.at[p, kind], recv_sem=r_recv.at[p, kind],
            device_id=to, device_id_type=MESH)

    def r_drain(p):
        for kind in range(6):
            rcopy(p, kind).wait_send()

    def partial(p, j, other, m):
        a, w = pieces[p]
        r = pl.ds(pl.multiple_of(m * half, half), half)
        return r, dot(hid[r, :], tdv[at.chunk(offs[j], other), :, a:a + w])

    def to_pair(p):
        a, w = pieces[p]
        for j in range(4):
            def tile(m, carry):
                r, v = partial(p, j, True, m)
                psend[j, r, a:a + w] = v.astype(BF16)
                return carry

            lax.fori_loop(0, 2, tile, 0)
            rcopy(p, j).start()

    def summed(p, j, adds, store):
        a, w = pieces[p]
        rcopy(p, j).wait_recv()

        def tile(m, carry):
            r, v = partial(p, j, False, m)
            v += precv[j, r, a:a + w].astype(F32)
            for k in adds:
                v += rrecv[k, r, a:a + w].astype(F32)
            store(r, v.astype(BF16))
            return carry

        lax.fori_loop(0, 2, tile, 0)

    def near(p):
        a, w = pieces[p]
        for j in (0, 1):
            def store(r, v):
                rsend[j, r, a:a + w] = v

            summed(p, j, (), store)
            rcopy(p, 4 + j).start()

    back = AllToAll(at, experts, cap, fin, ret, a_sem.at[0], a_sem.at[1], pieces)

    def home(p):
        a, w = pieces[p]

        def store_far(r, v):
            fin[1 - at.h, r, a:a + w] = v

        def store_own(r, v):
            fin[at.h, r, a:a + w] = v

        summed(p, 2, (), store_far)
        rcopy(p, 4).wait_recv()
        rcopy(p, 5).wait_recv()
        summed(p, 3, (0, 1), store_own)
        back.start(p)
        for h in range(2):
            ret[h, mine, a:a + w] = fin[h, mine, a:a + w]

    def tcopy(p):
        a, w = pieces[p]
        return pltpu.make_async_remote_copy(
            src_ref=tsend.at[:, :, pl.ds(a, w)], dst_ref=trecv.at[:, :, pl.ds(a, w)],
            send_sem=r_send.at[p, 6], recv_sem=r_recv.at[p, 6],
            device_id=at.to(2), device_id_type=MESH)

    def combine(p):
        a, w = pieces[p]
        back.wait(p)
        for h in range(2):
            got = ret[h, :, a:a + w]
            tsend[h, :, a:a + w] = (dot(comb_hi[...], got) + dot(comb_lo[...], got)).astype(BF16)
        tcopy(p).start()

    out_w = AllToAll(
        at, experts, cap, wsend, wbuf.at[at.c, at.b], a_sem.at[2], a_sem.at[3], pieces)
    out_v = Gather(at, wbuf, g_send, g_recv, pieces)

    def weigh(p):
        a, w = pieces[p]
        tcopy(p).wait_recv()
        both = []
        for h in range(2):
            total = tsend[h, :, a:a + w].astype(F32) + trecv[h, :, a:a + w].astype(F32)
            both.append(total.astype(BF16))
            for m in range(2):
                r = pl.ds(m * half, half)
                wsend[h, r, a:a + w] = (dot(sel[r, :], both[h]) * gsl[r, :]).astype(BF16)
        out_w.start(p)
        tan_ref[:, a:a + w] = jnp.where(at.h == 0, both[0], both[1])
        for h in range(2):
            wbuf[at.c, at.b, h, mine, a:a + w] = wsend[h, mine, a:a + w]

    def w_one(p):
        out_w.wait(p)
        out_v.one(p)

    def out_copy(p, k):
        a, w = pieces[p]
        return pltpu.make_async_copy(
            gnv.at[k, :, pl.ds(a, w)], gn_ref.at[0, :, pl.ds(k * chunk + a, w)], out_sem.at[p, k])

    def out_drain(p):
        for k in range(8):
            out_copy(p, k).wait()

    def product(p):
        a, w = pieces[p]
        if p == 0:
            hid_t[...] = hid[...].astype(F32).T.astype(BF16)
        out_v.done(p)
        for k in range(8):
            gnv[k, :, a:a + w] = dot(hid_t[...], wbuf[*cbh(k), :, a:a + w])
            out_copy(p, k).start()

    def t_drain(p):
        tcopy(p).wait_send()

    stages = [to_pair, near, home, combine, weigh, w_one, out_v.two, product]
    if upto is not None:
        stages = stages[:upto]
    if stages:
        in_steps(n, stages)
    ends = {1: r_drain, 3: back.drain, 4: t_drain, 5: out_w.drain, 7: out_v.drain, 8: out_drain}
    drains += [(end, n) for stage, end in ends.items() if len(stages) >= stage]
    for drain, count in drains:
        for p in range(count):
            drain(p)


def on_device(xwidths, widths, cap, upto, tokens, w_gate, w_up, tangent_down, gates, expert_ids):
    experts = lax.axis_size("ep")
    toks, width = tokens.shape
    chunk = width // 8
    hidden = w_gate.shape[2]
    rows = experts * cap
    xpieces, pieces = spans(xwidths), spans(widths)
    nx, n = len(xpieces), len(pieces)
    vmem, anywhere = pl.BlockSpec(memory_space=pltpu.VMEM), pl.BlockSpec(memory_space=pl.ANY)
    gn, tangent = pl.pallas_call(
        functools.partial(kernel, xpieces, pieces, experts, cap, upto),
        out_shape=(
            jax.ShapeDtypeStruct((1, hidden, width), F32),
            jax.ShapeDtypeStruct((toks, chunk), BF16),
        ),
        in_specs=[vmem, vmem, anywhere, anywhere, anywhere, anywhere],
        out_specs=(anywhere, vmem),
        scratch_shapes=[
            pltpu.VMEM((2, toks, chunk), BF16),
            pltpu.VMEM((width, hidden), BF16),
            pltpu.VMEM((width, hidden), BF16),
            pltpu.VMEM((8, hidden, chunk), BF16),
            pltpu.VMEM((rows, toks), BF16),
            pltpu.VMEM((rows, toks), F32),
            pltpu.VMEM((rows, 1), F32),
            pltpu.VMEM((toks, rows), BF16),
            pltpu.VMEM((toks, rows), BF16),
            pltpu.VMEM((2, rows, chunk), BF16),
            pltpu.VMEM((2, 2, 2, rows, chunk), BF16),
            pltpu.VMEM((rows, hidden), F32),
            pltpu.VMEM((rows, hidden), F32),
            pltpu.VMEM((rows, hidden), BF16),
            pltpu.VMEM((hidden, rows), BF16),
            pltpu.VMEM((4, rows, chunk), BF16),
            pltpu.VMEM((4, rows, chunk), BF16),
            pltpu.VMEM((2, rows, chunk), BF16),
            pltpu.VMEM((2, rows, chunk), BF16),
            pltpu.VMEM((2, rows, chunk), BF16),
            pltpu.VMEM((2, rows, chunk), BF16),
            pltpu.VMEM((2, toks, chunk), BF16),
            pltpu.VMEM((2, toks, chunk), BF16),
            pltpu.VMEM((2, rows, chunk), BF16),
            pltpu.VMEM((2, 2, 2, rows, chunk), BF16),
            pltpu.VMEM((8, hidden, chunk), F32),
            pltpu.SemaphoreType.DMA((12,)),
            pltpu.SemaphoreType.DMA((2, nx)),
            pltpu.SemaphoreType.DMA((4, n)),
            pltpu.SemaphoreType.DMA((nx, 5)),
            pltpu.SemaphoreType.DMA((nx, 5)),
            pltpu.SemaphoreType.DMA((n, 5)),
            pltpu.SemaphoreType.DMA((n, 5)),
            pltpu.SemaphoreType.DMA((n, 7)),
            pltpu.SemaphoreType.DMA((n, 7)),
            pltpu.SemaphoreType.DMA((n, 8)),
        ],
        compiler_params=pltpu.CompilerParams(
            collective_id=0, has_side_effects=True, vmem_limit_bytes=60 * 2**20),
    )(expert_ids.T, gates.T, tokens, w_gate, w_up, tangent_down)
    return gn, tangent


def solution(mesh, xwidths=(128,) * 7, widths=(128,) * 7, cap=32, upto=None):
    in_specs = (
        P("ep", None),
        P("ep", None, "fsdp"),
        P("ep", None, "fsdp"),
        P("ep", "fsdp", None),
        P("ep", None),
        P("ep", None),
    )
    out_specs = (P("ep", "fsdp", None), P("ep", "fsdp"))
    return jax.shard_map(
        functools.partial(on_device, xwidths, widths, cap, upto),
        mesh=mesh, in_specs=in_specs, out_specs=out_specs, check_vma=False,
    )
```

time: 140 us -> 122 us (0.87)
  Pallas kernels: 129 us -> 113 us
  local copies, waits for them, and re-layouts: 10.5 us -> 7.66 us
    pallas_call x1, Pallas kernels: 129 us -> 113 us  [on_device(): pl.pallas_call(functools.partial(kernel, xpieces, pieces, experts, cap, u...]
    unnamed x6 -> x4, local copies, waits for them, and re-layouts: 10.5 us -> 7.66 us
where the time goes in v2:
time: 122 us; the launch traced here: 121 us
  Pallas kernels  113 us (93%)
  local copies, waits for them, and re-layouts  7.66 us (6%)
    pallas_call x1, Pallas kernels, on_device(): pl.pallas_call(functools.partial(kernel, xpieces, pieces, experts, cap, u...  113 us
    unnamed x4, local copies, waits for them, and re-layouts  7.66 us

profile of v2, /device:TPU:1, one launch (start us, length us, event | category | flops | bytes accessed | tf_op | source)
XLA Modules:
  0.0 121.2 jit_solution(16686173183183399350)
XLA Ops:
  0.6 112.8 %shard_map.77 = (f32[1,256,7168]{2,1,0:T(8,128)}, bf16[128,896]{1,0:T(8,128)(2,1)}) custom-call(s32[2,128]{1,0:T(2,128)} %bitcast.2, f32[2,128]{1,0:T(2,128)} %bitcast.3, bf16[128,7168]{1,0:T(8,128)(2,1)} %tok_ref.1, bf16[1,7168,256]{2,1,0:T(8,128)(2,1)} %wg_ref.1, bf16[1,7168,256]{2,1,0:T(8,128)(2,1)} %wu_ref.1, bf16[1,256,7168]{2,1,0:T(8,128)(2,1)} %td_ref.1), custom_call_target="tpu_custom_call" | custom-call | tf_op jit(solution)/shard_map/pallas_call | solution.py:407
  113.5 0.0 copy-start
  113.5 7.0 %copy.10 = f32[1,256,7168]{2,1,0:T(8,128)} copy(f32[1,256,7168]{2,1,0:T(8,128)} %get-tuple-element.4) | data formatting | bytes 14680064
  120.5 0.0 copy-done
  120.5 0.7 copy.11
Async XLA Ops:
  113.5 7.0 %copy-start = (bf16[128,896]{1,0:T(8,128)(2,1)S(1)}, bf16[128,896]{1,0:T(8,128)(2,1)}, u32[]{:S(2)}) copy-start(bf16[128,896]{1,0:T(8,128)(2,1)} %get-tuple-element.5) | copy-start | bytes 688132

commit v3 on v0

v3 whole, which is shorter than its diff:
```python
import functools

import jax
import jax.numpy as jnp
from jax import lax
from jax.experimental import pallas as pl
from jax.experimental.pallas import tpu as pltpu
from jax.sharding import PartitionSpec as P

MESH = pl.DeviceIdType.MESH
F32 = jnp.float32
BF16 = jnp.bfloat16


def spans(widths):
    out, at = [], 0
    for w in widths:
        out.append((at, w))
        at += w
    return out


def dot(a, b):
    return jnp.dot(a, b, preferred_element_type=F32)


def wide(blocks):
    return jnp.concatenate(blocks, axis=1)


def cbh(k):
    return k % 2, k // 2 % 2, k // 4


class Place:
    def __init__(self):
        self.e = lax.axis_index("ep")
        self.f = lax.axis_index("fsdp")
        self.x = self.f // 2
        self.c = self.f - 2 * self.x
        self.h = self.x // 2
        self.b = self.x - 2 * self.h

    def chip(self, off):
        return lax.rem(self.x + off, 4)

    def chunk(self, off, other=False):
        return 2 * self.chip(off) + (1 - self.c if other else self.c)

    def to(self, off):
        return (self.e, self.chunk(off))

    def pair(self):
        return (self.e, self.chunk(0, True))


class AllToAll:
    def __init__(self, at, experts, cap, src, dst, send, recv):
        self.__dict__.update(locals())

    def start(self, i, groups, a, w):
        at, cap = self.at, self.cap

        def one(d, carry):
            to = lax.rem(at.e + d, self.experts)
            pltpu.make_async_remote_copy(
                src_ref=self.src.at[
                    :, groups, pl.ds(pl.multiple_of(to * cap, cap), cap), pl.ds(a, w)],
                dst_ref=self.dst.at[
                    :, groups, pl.ds(pl.multiple_of(at.e * cap, cap), cap), pl.ds(a, w)],
                send_sem=self.send.at[i],
                recv_sem=self.recv.at[i],
                device_id=(to, at.f),
                device_id_type=MESH,
            ).start()
            return carry

        lax.fori_loop(1, self.experts, one, 0)

    def _all(self, sem, i, groups, a, w):
        ref = self.src.at[:, groups, pl.ds(0, (self.experts - 1) * self.cap), pl.ds(a, w)]
        pltpu.make_async_copy(ref, ref, sem.at[i]).wait()

    def wait(self, *piece):
        self._all(self.recv, *piece)

    def drain(self, *piece):
        self._all(self.send, *piece)


class Gather:
    KINDS = 5

    def __init__(self, at, buf, send, recv):
        self.__dict__.update(locals())

    def copy(self, kind, i, groups, a, w):
        at = self.at
        cols = pl.ds(a, w)
        if kind == 2:
            ref = self.buf.at[at.c, at.b, :, groups, :, cols]
        elif kind < 2:
            ref = self.buf.at[at.c, at.b, at.h, groups, :, cols]
        else:
            ref = self.buf.at[at.c, 1 - at.b, at.chip(3 if kind == 3 else 1) // 2, groups, :, cols]
        to = (at.to(1), at.to(3), at.pair(), at.pair(), at.pair())[kind]
        return pltpu.make_async_remote_copy(
            src_ref=ref,
            dst_ref=ref,
            send_sem=self.send.at[i, kind],
            recv_sem=self.recv.at[i, kind],
            device_id=to,
            device_id_type=MESH,
        )

    def one(self, *piece):
        for kind in (0, 1, 2):
            self.copy(kind, *piece).start()

    def two(self, *piece):
        for kind in (0, 1):
            self.copy(kind, *piece).wait_recv()
            self.copy(kind + 3, *piece).start()

    def done(self, *piece):
        for kind in (2, 3, 4):
            self.copy(kind, *piece).wait_recv()

    def drain(self, *piece):
        for kind in range(self.KINDS):
            self.copy(kind, *piece).wait_send()


def plan(dwidths, rwidths):
    nd, nr = len(dwidths), len(rwidths)
    wd, wr = [w / 896 for w in dwidths], [w / 896 for w in rwidths]
    steps = {}
    for g in range(2):
        for p in range(nd):
            w, i = wd[p], g * nd + p
            steps["a", g, p] = (i, 1.2 * w, [], [("yz", 10 * w)])
            steps["1", g, p] = (i, 0.1, [("a", g, p)], [("x", 10 * w), ("pair", 2 * w)])
            steps["2", g, p] = (i, 0.1, [("1", g, p)], [("pair", 2 * w)])
            steps["u", g, p] = (90 + i, 2.4 * w, [("2", g, p)], [])
        steps["s", g, 0] = (100, 0.6, [("u", g, p) for p in range(nd)], [])
        for p in range(nr):
            w, i = wr[p], 20 + g * nr + p
            steps["t", g, p] = (i, 1.4 * w, [("s", g, 0)], [("pair", 4 * w)])
            steps["n", g, p] = (i, 1.2 * w, [("t", g, p)], [("x", 10 * w)])
            steps["h", g, p] = (i, 1.4 * w, [("n", g, p)], [("yz", 10 * w)])
    for p in range(nr):
        w, i = wr[p], 40 + p
        steps["c", 0, p] = (i, 1.4 * w, [("h", 0, p), ("h", 1, p)], [("x", 10 * w)])
        steps["w", 0, p] = (i, 1.6 * w, [("c", 0, p)], [("yz", 20 * w)])
        steps["3", 0, p] = (i, 0.1, [("w", 0, p)], [("x", 20 * w), ("pair", 4 * w)])
        steps["4", 0, p] = (i, 0.1, [("3", 0, p)], [("pair", 4 * w)])
        steps["p", 0, p] = (200 + i, 2.4 * w, [("4", 0, p)], [])
    delay = {"x": 2.5, "yz": 3.2, "pair": 2.0}
    now, free, there, order = 0.0, {"x": 0.0, "yz": 0.0, "pair": 0.0}, {}, []
    while len(order) < len(steps):
        left = [s for s in steps if s not in there and all(q in there for q in steps[s][2])]
        at = {s: max([there[q] for q in steps[s][2]], default=0.0) for s in left}
        ready = [s for s in left if at[s] <= now]
        if not ready:
            now = min(at.values())
            continue
        step = min(ready, key=lambda s: (steps[s][0], s))
        now += steps[step][1]
        there[step] = now
        for link, time in steps[step][3]:
            free[link] = max(free[link], now) + time
            there[step] = max(there[step], free[link] + delay[link])
        order.append(step)
    return order, now


def kernel(
    dwidths, rwidths, experts, cap, upto,
    ids_ref, gates_ref, tok_ref, wg_ref, wu_ref, td_ref,
    gn_ref, tan_ref,
    tokv, wgv, wuv, tdv, sel, selg, gsl, comb_hi, comb_lo, send, xbuf, acc_g, acc_u, hid, hid_t,
    psend, precv, rsend, rrecv, fin, ret, tsend, trecv, wsend, wbuf,
    load, x_sem, h_sem, w_sem, xg_send, xg_recv, g_send, g_recv, r_send, r_recv, t_sem,
):
    at = Place()
    dspans, rspans = spans(dwidths), spans(rwidths)
    nd, nr = len(dspans), len(rspans)
    toks, chunk = tokv.shape[1:]
    half = experts * cap
    ranks = 2 * cap
    both = slice(None)

    loads = [pltpu.make_async_copy(
        tok_ref.at[:, pl.ds(pl.multiple_of((4 * h + 2 * at.b + at.c) * chunk, 128), chunk)],
        tokv.at[h], load.at[h]) for h in range(2)]
    loads += [pltpu.make_async_copy(wg_ref.at[0], wgv, load.at[2]),
              pltpu.make_async_copy(wu_ref.at[0], wuv, load.at[3])]
    loads += [pltpu.make_async_copy(
        td_ref.at[0, :, pl.ds(k * chunk, chunk)], tdv.at[k], load.at[4 + k]) for k in range(8)]
    for copy in loads:
        copy.start()

    barrier = pltpu.get_barrier_semaphore()

    def greet(d, carry):
        pl.semaphore_signal(
            barrier, inc=1, device_id=(lax.rem(at.e + d, experts), at.f), device_id_type=MESH)
        return carry

    lax.fori_loop(1, experts, greet, 0)
    for to in (at.to(1), at.to(3), at.to(2), at.pair()):
        pl.semaphore_signal(barrier, inc=1, device_id=to, device_id_type=MESH)

    expert = lax.broadcasted_iota(jnp.int32, (experts, toks), 0)
    named = [ids_ref[k:k + 1, :] == expert for k in range(ids_ref.shape[0])]
    mask_t = sum(jnp.where(m, 1.0, 0.0) for m in named)
    gate_t = sum(jnp.where(m, gates_ref[k:k + 1, :], 0.0) for k, m in enumerate(named))
    earlier = jnp.where(
        lax.broadcasted_iota(jnp.int32, (toks, toks), 0)
        < lax.broadcasted_iota(jnp.int32, (toks, toks), 1), 1.0, 0.0)
    rank_t = dot(mask_t.astype(BF16), earlier.astype(BF16))
    place = lax.broadcasted_iota(jnp.int32, (ranks, toks), 0).astype(F32)
    for k in range(experts):
        here = (rank_t[k:k + 1, :] == place) & (mask_t[k:k + 1, :] > 0.5)
        picked = jnp.where(here, gate_t[k:k + 1, :], 0.0)
        one = jnp.where(here, 1.0, 0.0).astype(BF16)
        total = jnp.sum(picked, axis=1, keepdims=True)
        for g in range(2):
            r, part = slice(k * cap, (k + 1) * cap), slice(g * cap, (g + 1) * cap)
            sel[g, r, :] = one[part]
            selg[g, r, :] = picked[part]
            gsl[g, r, :] = total[part]

    mine = pl.ds(pl.multiple_of(at.e * cap, cap), cap)
    out_a = AllToAll(at, experts, cap, send, xbuf.at[at.c, at.b], x_sem.at[0], x_sem.at[1])
    out_g = Gather(at, xbuf, xg_send, xg_recv)
    back = AllToAll(at, experts, cap, fin, ret, h_sem.at[0], h_sem.at[1])
    out_w = AllToAll(at, experts, cap, wsend, wbuf.at[at.c, at.b], w_sem.at[0], w_sem.at[1])
    out_v = Gather(at, wbuf, g_send, g_recv)

    def dpiece(g, p):
        return g * nd + p, pl.ds(g, 1), *dspans[p]

    def rpiece(g, p):
        return g * nr + p, pl.ds(g, 1), *rspans[p]

    def wpiece(p):
        return p, both, *rspans[p]

    def choose(g, p):
        a, w = dspans[p]
        rows = dot(sel[g], wide([tokv[h, :, a:a + w] for h in range(2)])).astype(BF16)
        for h in range(2):
            send[h, g, :, a:a + w] = rows[:, h * w:(h + 1) * w]
        out_a.start(*dpiece(g, p))
        for h in range(2):
            xbuf[at.c, at.b, h, g, mine, a:a + w] = send[h, g, mine, a:a + w]

    def d_one(g, p):
        out_a.wait(*dpiece(g, p))
        out_g.one(*dpiece(g, p))

    def d_two(g, p):
        out_g.two(*dpiece(g, p))

    def up(g, p):
        a, w = dspans[p]
        if (g, p) == (0, 0):
            loads[2].wait()
            loads[3].wait()
        out_g.done(*dpiece(g, p))
        for acc, weights in ((acc_g, wgv), (acc_u, wuv)):
            total = None if p == 0 else acc[g]
            for k in range(0, 8, 2):
                c, b, h = cbh(k)
                part = dot(
                    wide([xbuf[c, b, h, g, :, a:a + w] for c in range(2)]),
                    jnp.concatenate([
                        weights[q * chunk + a:q * chunk + a + w, :] for q in (k, k + 1)], axis=0))
                total = part if total is None else total + part
            acc[g] = total

    def silu(g, _):
        def tile(m, carry):
            r = pl.ds(pl.multiple_of(m * ranks, ranks), ranks)
            v = acc_g[g, r, :]
            hid[g, r, :] = (v / (1.0 + jnp.exp(-v)) * acc_u[g, r, :]).astype(BF16)
            return carry

        lax.fori_loop(0, half // ranks, tile, 0)
        hid_t[g] = hid[g].astype(F32).T.astype(BF16)
        if g == 0:
            for copy in loads[4:]:
                copy.wait()

    offs = (1, 3, 2, 0)

    def rcopy(kind, g, p):
        a, w = rspans[p]
        if kind < 4:
            src, dst, to = psend.at[kind], precv.at[kind], at.pair()
        else:
            src, dst, to = rsend.at[kind - 4], rrecv.at[kind - 4], at.to(1 if kind == 4 else 3)
        return pltpu.make_async_remote_copy(
            src_ref=src.at[g, :, pl.ds(a, w)], dst_ref=dst.at[g, :, pl.ds(a, w)],
            send_sem=r_send.at[g * nr + p, kind], recv_sem=r_recv.at[g * nr + p, kind],
            device_id=to, device_id_type=MESH)

    def partial(g, p, js, other):
        a, w = rspans[p]
        v = dot(hid[g], wide([tdv[at.chunk(offs[j], other), :, a:a + w] for j in js]))
        return [v[:, i * w:(i + 1) * w] for i in range(len(js))]

    def to_pair(g, p):
        a, w = rspans[p]
        for js in ((0, 1), (2, 3)):
            for j, v in zip(js, partial(g, p, js, True)):
                psend[j, g, :, a:a + w] = v.astype(BF16)
                rcopy(j, g, p).start()

    def summed(g, p, js):
        a, w = rspans[p]
        for j, v in zip(js, partial(g, p, js, False)):
            rcopy(j, g, p).wait_recv()
            yield v + precv[j, g, :, a:a + w].astype(F32)

    def near(g, p):
        a, w = rspans[p]
        for j, v in enumerate(summed(g, p, (0, 1))):
            rsend[j, g, :, a:a + w] = v.astype(BF16)
            rcopy(4 + j, g, p).start()

    def home(g, p):
        a, w = rspans[p]
        far, v = summed(g, p, (2, 3))
        fin[1 - at.h, g, :, a:a + w] = far.astype(BF16)
        for k in range(2):
            rcopy(4 + k, g, p).wait_recv()
            v += rrecv[k, g, :, a:a + w].astype(F32)
        fin[at.h, g, :, a:a + w] = v.astype(BF16)
        back.start(*rpiece(g, p))
        for h in range(2):
            ret[h, g, mine, a:a + w] = fin[h, g, mine, a:a + w]

    def tcopy(p):
        a, w = rspans[p]
        return pltpu.make_async_remote_copy(
            src_ref=tsend.at[:, :, pl.ds(a, w)], dst_ref=trecv.at[:, :, pl.ds(a, w)],
            send_sem=t_sem.at[0, p], recv_sem=t_sem.at[1, p],
            device_id=at.to(2), device_id_type=MESH)

    def combine(_, p):
        a, w = rspans[p]
        if p == 0:
            for g in range(2):
                comb = selg[g].T
                hi = comb.astype(BF16)
                comb_hi[g] = hi
                comb_lo[g] = (comb - hi.astype(F32)).astype(BF16)
        for g in range(2):
            back.wait(*rpiece(g, p))
        total = jnp.zeros((toks, 2 * w), F32)
        for g in range(2):
            got = wide([ret[h, g, :, a:a + w] for h in range(2)])
            total += dot(comb_hi[g], got) + dot(comb_lo[g], got)
        for h in range(2):
            tsend[h, :, a:a + w] = total[:, h * w:(h + 1) * w].astype(BF16)
        tcopy(p).start()

    def weigh(_, p):
        a, w = rspans[p]
        tcopy(p).wait_recv()
        tangents = []
        for h in range(2):
            total = tsend[h, :, a:a + w].astype(F32) + trecv[h, :, a:a + w].astype(F32)
            tangents.append(total.astype(BF16))
        for g in range(2):
            rows = (dot(sel[g], wide(tangents)) * gsl[g]).astype(BF16)
            for h in range(2):
                wsend[h, g, :, a:a + w] = rows[:, h * w:(h + 1) * w]
        out_w.start(*wpiece(p))
        tan_ref[:, a:a + w] = jnp.where(at.h == 0, tangents[0], tangents[1])
        for h in range(2):
            for g in range(2):
                wbuf[at.c, at.b, h, g, mine, a:a + w] = wsend[h, g, mine, a:a + w]

    def w_one(_, p):
        out_w.wait(*wpiece(p))
        out_v.one(*wpiece(p))

    def w_two(_, p):
        out_v.two(*wpiece(p))

    def product(_, p):
        a, w = rspans[p]
        out_v.done(*wpiece(p))
        for k in range(0, 8, 2):
            c, b, h = cbh(k)
            v = sum(dot(hid_t[g], wide([wbuf[c, b, h, g, :, a:a + w] for c in range(2)]))
                    for g in range(2))
            for c in range(2):
                gn_ref[0, :, (k + c) * chunk + a:(k + c) * chunk + a + w] = v[:, c * w:(c + 1) * w]

    loads[0].wait()
    loads[1].wait()
    pl.semaphore_wait(barrier, experts - 1 + 4)
    steps = {
        "a": choose, "1": d_one, "2": d_two, "u": up, "s": silu, "t": to_pair, "n": near,
        "h": home, "c": combine, "w": weigh, "3": w_one, "4": w_two, "p": product}
    for kind, g, p in plan(dwidths, rwidths)[0]:
        if upto is None or kind in upto:
            steps[kind](g, p)

    for g in range(2):
        for p in range(nd):
            out_a.drain(*dpiece(g, p))
            out_g.drain(*dpiece(g, p))
    if upto is None:
        for p in range(nr):
            for g in range(2):
                back.drain(*rpiece(g, p))
                for kind in range(6):
                    rcopy(kind, g, p).wait_send()
            tcopy(p).wait_send()
            out_w.drain(*wpiece(p))
            out_v.drain(*wpiece(p))


def on_device(dwidths, rwidths, cap, upto, tokens, w_gate, w_up, tangent_down, gates, expert_ids):
    experts = lax.axis_size("ep")
    toks, width = tokens.shape
    chunk = width // 8
    hidden = w_gate.shape[2]
    half = experts * cap
    nd, nr = len(dwidths), len(rwidths)
    vmem, anywhere = pl.BlockSpec(memory_space=pltpu.VMEM), pl.BlockSpec(memory_space=pl.ANY)
    return pl.pallas_call(
        functools.partial(kernel, dwidths, rwidths, experts, cap, upto),
        out_shape=(
            pltpu.VMEM((1, hidden, width), F32),
            pltpu.VMEM((toks, chunk), BF16),
        ),
        in_specs=[vmem, vmem, anywhere, anywhere, anywhere, anywhere],
        out_specs=(vmem, vmem),
        scratch_shapes=[
            pltpu.VMEM((2, toks, chunk), BF16),
            pltpu.VMEM((width, hidden), BF16),
            pltpu.VMEM((width, hidden), BF16),
            pltpu.VMEM((8, hidden, chunk), BF16),
            pltpu.VMEM((2, half, toks), BF16),
            pltpu.VMEM((2, half, toks), F32),
            pltpu.VMEM((2, half, 1), F32),
            pltpu.VMEM((2, toks, half), BF16),
            pltpu.VMEM((2, toks, half), BF16),
            pltpu.VMEM((2, 2, half, chunk), BF16),
            pltpu.VMEM((2, 2, 2, 2, half, chunk), BF16),
            pltpu.VMEM((2, half, hidden), F32),
            pltpu.VMEM((2, half, hidden), F32),
            pltpu.VMEM((2, half, hidden), BF16),
            pltpu.VMEM((2, hidden, half), BF16),
            pltpu.VMEM((4, 2, half, chunk), BF16),
            pltpu.VMEM((4, 2, half, chunk), BF16),
            pltpu.VMEM((2, 2, half, chunk), BF16),
            pltpu.VMEM((2, 2, half, chunk), BF16),
            pltpu.VMEM((2, 2, half, chunk), BF16),
            pltpu.VMEM((2, 2, half, chunk), BF16),
            pltpu.VMEM((2, toks, chunk), BF16),
            pltpu.VMEM((2, toks, chunk), BF16),
            pltpu.VMEM((2, 2, half, chunk), BF16),
            pltpu.VMEM((2, 2, 2, 2, half, chunk), BF16),
            pltpu.SemaphoreType.DMA((12,)),
            pltpu.SemaphoreType.DMA((2, 2 * nd)),
            pltpu.SemaphoreType.DMA((2, 2 * nr)),
            pltpu.SemaphoreType.DMA((2, nr)),
            pltpu.SemaphoreType.DMA((2 * nd, 5)),
            pltpu.SemaphoreType.DMA((2 * nd, 5)),
            pltpu.SemaphoreType.DMA((nr, 5)),
            pltpu.SemaphoreType.DMA((nr, 5)),
            pltpu.SemaphoreType.DMA((2 * nr, 6)),
            pltpu.SemaphoreType.DMA((2 * nr, 6)),
            pltpu.SemaphoreType.DMA((2, nr)),
        ],
        compiler_params=pltpu.CompilerParams(
            collective_id=0, has_side_effects=True, vmem_limit_bytes=50 * 2**20),
    )(expert_ids.T, gates.T, tokens, w_gate, w_up, tangent_down)


def solution(mesh, dwidths=(128, 256, 256, 256), rwidths=(128,) * 7, cap=16, upto=None):
    in_specs = (
        P("ep", None),
        P("ep", None, "fsdp"),
        P("ep", None, "fsdp"),
        P("ep", "fsdp", None),
        P("ep", None),
        P("ep", None),
    )
    out_specs = (P("ep", "fsdp", None), P("ep", "fsdp"))
    return jax.shard_map(
        functools.partial(on_device, dwidths, rwidths, cap, upto),
        mesh=mesh, in_specs=in_specs, out_specs=out_specs, check_vma=False,
    )
```

time: 512 us -> 102 us (0.20)
  waiting for transfers between devices: 271 us -> 0 us
  Pallas kernels: 0 us -> 97.1 us
  blocking collectives: 90.4 us -> 0 us
  local copies, waits for them, and re-layouts: 56 us -> 3.74 us
  other arithmetic: 36.6 us -> 0 us
  matrix products: 22 us -> 0 us
  starting transfers between devices: 21 us -> 0 us
  between operations: 14.2 us -> 0.64 us
    all_to_all x3 -> x0, waiting for transfers between devices: 211 us -> none  [the longest x1 107 us: on_device(): lax.all_to_all(outgoing, 'ep', split_axis=0, concat_axis=0, tiled=True)]
    pallas_call x0 -> x1, Pallas kernels: none -> 97.1 us  [on_device(): pl.pallas_call(functools.partial(kernel, dwidths, rwidths, experts, cap,...]
    all_to_all x1 -> x0, blocking collectives: 90.4 us -> none  [on_device(): lax.all_to_all(weighted, 'ep', split_axis=0, concat_axis=0, tiled=True)]
    gather x3 -> x0, local copies, waits for them, and re-layouts: 36.7 us -> none  [the longest x1 15.5 us: on_device(): jnp.take(whole, slot_token, axis=0, mode='fill', fill_value=0)]
    unnamed x3 -> x0, waiting for transfers between devices: 32.4 us -> none
    all_gather x1 -> x0, waiting for transfers between devices: 27.7 us -> none  [on_device(): whole = lax.all_gather(tangent_sum, 'fsdp', axis=1, tiled=True)]
    dot_general x4 -> x0, matrix products: 22 us -> none  [the longest x1 6.33 us: on_device(): first = jnp.dot(flat_rows, w_gate[0], preferred_element_type=jnp.float32)]
    all_to_all x3 -> x0, starting transfers between devices: 20.5 us -> none  [the longest x1 8.6 us: on_device(): lax.all_to_all(slot_gate.reshape(experts, capacity).astype(jnp.bfloat16),...]
  transfers between devices with their start and end apart: 5 -> 0, of which waited for: 4 -> 0; matrix products, arithmetic and copies ran while one was open for 3% -> 0% of each run, Pallas kernels for 0% -> 0%
where the time goes in v3:
time: 102 us
  Pallas kernels  97.1 us (95%)
  local copies, waits for them, and re-layouts  3.74 us (4%)
    pallas_call x1, Pallas kernels, on_device(): pl.pallas_call(functools.partial(kernel, dwidths, rwidths, experts, cap,...  97.1 us
    unnamed x2, local copies, waits for them, and re-layouts  3.74 us

profile of v3, /device:TPU:1, one launch (start us, length us, event | category | flops | bytes accessed | tf_op | source)
XLA Modules:
  0.0 101.5 jit_solution(10746414525391385283)
XLA Ops:
  0.6 97.1 %shard_map.77 = (f32[1,256,7168]{2,1,0:T(8,128)S(1)}, bf16[128,896]{1,0:T(8,128)(2,1)S(1)}) custom-call(s32[2,128]{1,0:T(2,128)} %bitcast.2, f32[2,128]{1,0:T(2,128)} %bitcast.3, bf16[128,7168]{1,0:T(8,128)(2,1)} %tok_ref.1, bf16[1,7168,256]{2,1,0:T(8,128)(2,1)} %wg_ref.1, bf16[1,7168,256]{2,1,0:T(8,128)(2,1)} %wu_ref.1, bf16[1,256,7168]{2,1,0:T(8,128)(2,1)} %td_ref.1), custom_call_target="tpu_custom_call" | custom-call | tf_op jit(solution)/shard_map/pallas_call | solution.py:437
  97.8 3.1 %copy.10 = f32[1,256,7168]{2,1,0:T(8,128)} copy(f32[1,256,7168]{2,1,0:T(8,128)S(1)} %get-tuple-element.2) | data formatting | bytes 14680064
  100.8 0.7 copy.11

commit v4 on v3

v4 whole, which is shorter than its diff:
```python
import functools

import jax
import jax.numpy as jnp
from jax import lax
from jax.experimental import pallas as pl
from jax.experimental.pallas import tpu as pltpu
from jax.sharding import PartitionSpec as P

MESH = pl.DeviceIdType.MESH
F32 = jnp.float32
BF16 = jnp.bfloat16


def spans(widths):
    out, at = [], 0
    for w in widths:
        out.append((at, w))
        at += w
    return out


def dot(a, b):
    return jnp.dot(a, b, preferred_element_type=F32)


def wide(blocks):
    return jnp.concatenate(blocks, axis=1)


def cbh(k):
    return k % 2, k // 2 % 2, k // 4


class Place:
    def __init__(self):
        self.e = lax.axis_index("ep")
        self.f = lax.axis_index("fsdp")
        self.x = self.f // 2
        self.c = self.f - 2 * self.x
        self.h = self.x // 2
        self.b = self.x - 2 * self.h

    def chip(self, off):
        return lax.rem(self.x + off, 4)

    def chunk(self, off, other=False):
        return 2 * self.chip(off) + (1 - self.c if other else self.c)

    def to(self, off):
        return (self.e, self.chunk(off))

    def pair(self):
        return (self.e, self.chunk(0, True))


class AllToAll:
    def __init__(self, at, experts, cap, src, dst, sems):
        self.__dict__.update(locals())

    def start(self, i, lead, a, w):
        at, cap = self.at, self.cap

        def one(d, carry):
            to = lax.rem(at.e + d, self.experts)
            there = pl.ds(pl.multiple_of(to * cap, cap), cap)
            here = pl.ds(pl.multiple_of(at.e * cap, cap), cap)
            pltpu.make_async_remote_copy(
                src_ref=self.src.at[(*lead, there, pl.ds(a, w))],
                dst_ref=self.dst.at[(*lead, here, pl.ds(a, w))],
                send_sem=self.sems.at[0, i],
                recv_sem=self.sems.at[1, i],
                device_id=(to, at.f),
                device_id_type=MESH,
            ).start()
            return carry

        lax.fori_loop(1, self.experts, one, 0)

    def _all(self, way, i, lead, a, w):
        ref = self.src.at[(*lead, pl.ds(0, (self.experts - 1) * self.cap), pl.ds(a, w))]
        pltpu.make_async_copy(ref, ref, self.sems.at[way, i]).wait()

    def wait(self, *piece):
        self._all(1, *piece)

    def drain(self, *piece):
        self._all(0, *piece)


class Gather:
    def __init__(self, at, buf, send, recv):
        self.__dict__.update(locals())

    def copy(self, kind, i, groups, a, w):
        at = self.at
        ref = self.buf.at[at.b, at.h, groups, :, pl.ds(a, w)]
        return pltpu.make_async_remote_copy(
            src_ref=ref,
            dst_ref=ref,
            send_sem=self.send.at[i, kind],
            recv_sem=self.recv.at[i, kind],
            device_id=at.to(1 if kind == 0 else 3),
            device_id_type=MESH,
        )

    def start(self, *piece):
        for kind in range(2):
            self.copy(kind, *piece).start()

    def wait(self, *piece):
        for kind in range(2):
            self.copy(kind, *piece).wait_recv()

    def drain(self, *piece):
        for kind in range(2):
            self.copy(kind, *piece).wait_send()


def plan(dwidths, rwidths, direct, delay=(3.0, 4.0, 2.5)):
    nd, nr = len(dwidths), len(rwidths)
    wd, wr = [w / 896 for w in dwidths], [w / 896 for w in rwidths]
    delay = dict(zip(("x", "yz", "pair"), delay))
    steps = {}
    for g in range(2):
        for p in range(nd):
            w, i = wd[p], g * nd + p
            if (g, p) in direct:
                steps["a", g, p] = (i, 0.4 + 2.4 * w, [], [("yz", 20 * w)])
                steps["u", g, p] = (90 + i, 2.4 * w, [("a", g, p), "weights"], [])
            else:
                steps["a", g, p] = (i, 0.4 + 1.2 * w, [], [("yz", 10 * w)])
                steps["1", g, p] = (i, 0.1, [("a", g, p)], [("x", 10 * w)])
                steps["u", g, p] = (90 + i, 2.4 * w, [("1", g, p), "weights"], [])
        steps["e", g, 0] = (99, 0.1, [("u", g, p) for p in range(nd)], [("pair", 2.0)])
        steps["s", g, 0] = (100, 1.0, [("e", g, 0)], [])
        for p in range(nr):
            w, i = wr[p], 20 + g * nr + p
            steps["n", g, p] = (i, 1.2 * w, [("s", g, 0)], [("x", 10 * w)])
            steps["h", g, p] = (i, 0.4 + 1.4 * w, [("n", g, p)], [("yz", 10 * w)])
    for p in range(nr):
        w, i = wr[p], 40 + p
        steps["c", 0, p] = (i, 1.4 * w, [("h", 0, p), ("h", 1, p)], [("x", 10 * w)])
        steps["w", 0, p] = (i, 0.4 + 1.6 * w, [("c", 0, p)], [("yz", 20 * w)])
        steps["3", 0, p] = (i, 0.1, [("w", 0, p)], [("x", 20 * w), ("pair", 4 * w)])
        steps["4", 0, p] = (i, 0.1, [("3", 0, p)], [("pair", 4 * w)])
        steps["p", 0, p] = (200 + i, 2.4 * w, [("4", 0, p)], [])
    now, free, order = 0.0, {"x": 0.0, "yz": 0.0, "pair": 0.0}, []
    there = {"weights": 11.0}
    while len(order) < len(steps):
        left = [s for s in steps if s not in there and all(q in there for q in steps[s][2])]
        at = {s: max([there[q] for q in steps[s][2]], default=0.0) for s in left}
        ready = [s for s in left if at[s] <= now]
        if not ready:
            now = min(at.values())
            continue
        step = min(ready, key=lambda s: (steps[s][0], s))
        now += steps[step][1]
        there[step] = now
        for link, time in steps[step][3]:
            free[link] = max(free[link], now) + time
            there[step] = max(there[step], free[link] + delay[link])
        order.append(step)
    return order, now


def kernel(
    dwidths, rwidths, direct, experts, cap, options,
    ids_hbm, gates_hbm, tok_ref, wg_ref, wu_ref, td_ref,
    gn_ref, tan_ref,
    ids_ref, gates_ref, tokv, wgv, wuv, tdv, sel, selg, gsl, comb_hi, comb_lo, send, xbuf, acc,
    acc_in, hid, hid_t, rsend, rrecv, fin, ret, tsend, trecv, wsend, wbuf,
    load, v_sem, x_sem, h_sem, w_sem, xg_send, xg_recv, g_send, g_recv, p_sem, e_sem, r_send,
    r_recv, t_sem,
):
    at = Place()
    dspans, rspans = spans(dwidths), spans(rwidths)
    nd, nr = len(dspans), len(rspans)
    toks, chunk = tokv.shape[2:]
    hidden = gn_ref.shape[1]
    half = experts * cap
    ranks = 2 * cap
    both = slice(None)
    chips = [(b, h) for h in range(2) for b in range(2)]

    barrier = pltpu.get_barrier_semaphore()

    def greet(d, carry):
        pl.semaphore_signal(
            barrier, inc=1, device_id=(lax.rem(at.e + d, experts), at.f), device_id_type=MESH)
        return carry

    lax.fori_loop(1, experts, greet, 0)
    for to in (at.to(1), at.to(3), at.to(2), at.pair()):
        pl.semaphore_signal(barrier, inc=1, device_id=to, device_id_type=MESH)

    def columns(x, c):
        return pl.ds(pl.multiple_of((2 * x + c) * chunk, 128), chunk)

    own = pl.ds(pl.multiple_of(at.c * hidden, 128), hidden)

    def weights(x, c):
        return [(wg_ref.at[0, columns(x, c), :], wgv.at[x, :, own]),
                (wu_ref.at[0, columns(x, c), :], wuv.at[x, :, own]),
                (td_ref.at[0, :, columns(x, c)], tdv.at[x, own, :])]

    loads = [pltpu.make_async_copy(ids_hbm, ids_ref, load.at[0]),
             pltpu.make_async_copy(gates_hbm, gates_ref, load.at[1])]
    loads += [pltpu.make_async_copy(
        tok_ref.at[:, columns(2 * h + b, at.c)], tokv.at[b, h], load.at[2 + 2 * h + b])
        for b, h in chips]
    local, shared = [], []
    for x in range(4):
        for k, (src, dst) in enumerate(weights(x, at.c)):
            local.append(pltpu.make_async_copy(src, dst, load.at[6 + 3 * x + k]))
        for k, (src, dst) in enumerate(weights(x, 1 - at.c)):
            shared.append(pltpu.make_async_remote_copy(
                src_ref=src, dst_ref=dst, send_sem=v_sem.at[0, 3 * x + k],
                recv_sem=v_sem.at[1, 3 * x + k], device_id=at.pair(), device_id_type=MESH))
    for copy in loads + local:
        copy.start()
    loads[0].wait()
    loads[1].wait()

    expert = lax.broadcasted_iota(jnp.int32, (experts, toks), 0)
    named = [ids_ref[k:k + 1, :] == expert for k in range(ids_ref.shape[0])]
    mask_t = sum(jnp.where(m, 1.0, 0.0) for m in named)
    gate_t = sum(jnp.where(m, gates_ref[k:k + 1, :], 0.0) for k, m in enumerate(named))
    earlier = jnp.where(
        lax.broadcasted_iota(jnp.int32, (toks, toks), 0)
        < lax.broadcasted_iota(jnp.int32, (toks, toks), 1), 1.0, 0.0)
    rank_t = dot(mask_t.astype(BF16), earlier.astype(BF16))
    place = lax.broadcasted_iota(jnp.int32, (ranks, toks), 0).astype(F32)
    for k in range(experts):
        here = (rank_t[k:k + 1, :] == place) & (mask_t[k:k + 1, :] > 0.5)
        picked = jnp.where(here, gate_t[k:k + 1, :], 0.0)
        one = jnp.where(here, 1.0, 0.0).astype(BF16)
        total = jnp.sum(picked, axis=1, keepdims=True)
        for g in range(2):
            r, part = slice(k * cap, (k + 1) * cap), slice(g * cap, (g + 1) * cap)
            sel[g, r, :] = one[part]
            selg[g, r, :] = picked[part]
            gsl[g, r, :] = total[part]

    mine = pl.ds(pl.multiple_of(at.e * cap, cap), cap)
    out_a = AllToAll(at, experts, cap, send, xbuf, x_sem)
    out_g = Gather(at, xbuf, xg_send, xg_recv)
    back = AllToAll(at, experts, cap, fin, ret, h_sem)
    out_w = AllToAll(at, experts, cap, wsend, wbuf.at[at.c], w_sem)
    out_v = Gather(at, wbuf.at[at.c], g_send, g_recv)

    def apiece(g, p):
        lead = (both, both, g) if (g, p) in direct else (at.b, both, g)
        return g * nd + p, lead, *dspans[p]

    def xpiece(g, p):
        return g * nd + p, g, *dspans[p]

    def hpiece(g, p):
        return g * nr + p, (both, g), *rspans[p]

    def wpiece(p):
        return p, (at.b, both, both), *rspans[p]

    def vpiece(p):
        return p, both, *rspans[p]

    def choose(g, p):
        a, w = dspans[p]
        if (g, p) in direct:
            which = [(b, h) for b, h in chips]
        else:
            which = [(at.b, h) for h in range(2)]
        rows = dot(sel[g], wide([tokv[b, h, :, a:a + w] for b, h in which])).astype(BF16)
        for k, (b, h) in enumerate(which):
            send[b, h, g, :, a:a + w] = rows[:, k * w:(k + 1) * w]
        out_a.start(*apiece(g, p))
        for b, h in which:
            xbuf[b, h, g, mine, a:a + w] = send[b, h, g, mine, a:a + w]

    def d_one(g, p):
        out_a.wait(*apiece(g, p))
        out_g.start(*xpiece(g, p))

    def up(g, p):
        a, w = dspans[p]
        if (g, p) == first_up:
            for x in range(4):
                for k in range(2):
                    local[3 * x + k].wait()
                    shared[3 * x + k].wait_recv()
        if (g, p) in direct:
            out_a.wait(*apiece(g, p))
        else:
            out_g.wait(*xpiece(g, p))
        for n, matrix in enumerate((wgv, wuv)):
            cols = slice(n * 2 * hidden, (n + 1) * 2 * hidden)
            total = None if up_seen[g] == 0 else acc[g, :, cols]
            for h in range(2):
                part = dot(
                    wide([xbuf[b, h, g, :, a:a + w] for b in range(2)]),
                    jnp.concatenate([matrix[2 * h + b, a:a + w, :] for b in range(2)], axis=0))
                total = part if total is None else total + part
            acc[g, :, cols] = total
        up_seen[g] += 1

    def ecopy(g):
        return pltpu.make_async_remote_copy(
            src_ref=acc.at[g], dst_ref=acc_in.at[g], send_sem=e_sem.at[0, g],
            recv_sem=e_sem.at[1, g], device_id=at.pair(), device_id_type=MESH)

    def exchange(g, _):
        ecopy(g).start()

    def silu(g, _):
        ecopy(g).wait_recv()

        def tile(m, carry):
            r = pl.ds(pl.multiple_of(m * cap, cap), cap)
            v = acc[g, r, :] + acc_in[g, r, :]
            gate, value = v[:, :2 * hidden], v[:, 2 * hidden:]
            hid[g, r, :] = (gate / (1.0 + jnp.exp(-gate)) * value).astype(BF16)
            return carry

        lax.fori_loop(0, half // cap, tile, 0)
        if g == 0:
            for x in range(4):
                local[3 * x + 2].wait()
                shared[3 * x + 2].wait_recv()

    offs = (1, 3, 2, 0)

    def rcopy(kind, g, p):
        a, w = rspans[p]
        return pltpu.make_async_remote_copy(
            src_ref=rsend.at[kind, g, :, pl.ds(a, w)], dst_ref=rrecv.at[kind, g, :, pl.ds(a, w)],
            send_sem=r_send.at[g * nr + p, kind], recv_sem=r_recv.at[g * nr + p, kind],
            device_id=at.to(1 if kind == 0 else 3), device_id_type=MESH)

    def partial(g, p, js):
        a, w = rspans[p]
        v = dot(hid[g], wide([tdv[at.chip(offs[j]), :, a:a + w] for j in js]))
        return [v[:, i * w:(i + 1) * w] for i in range(len(js))]

    def near(g, p):
        a, w = rspans[p]
        for j, v in enumerate(partial(g, p, (0, 1))):
            rsend[j, g, :, a:a + w] = v.astype(BF16)
            rcopy(j, g, p).start()

    def home(g, p):
        a, w = rspans[p]
        far, v = partial(g, p, (2, 3))
        fin[1 - at.h, g, :, a:a + w] = far.astype(BF16)
        for k in range(2):
            rcopy(k, g, p).wait_recv()
            v += rrecv[k, g, :, a:a + w].astype(F32)
        fin[at.h, g, :, a:a + w] = v.astype(BF16)
        back.start(*hpiece(g, p))
        for h in range(2):
            ret[h, g, mine, a:a + w] = fin[h, g, mine, a:a + w]

    def tcopy(p):
        a, w = rspans[p]
        return pltpu.make_async_remote_copy(
            src_ref=tsend.at[:, :, pl.ds(a, w)], dst_ref=trecv.at[:, :, pl.ds(a, w)],
            send_sem=t_sem.at[0, p], recv_sem=t_sem.at[1, p],
            device_id=at.to(2), device_id_type=MESH)

    def combine(_, p):
        a, w = rspans[p]
        if p == 0:
            for g in range(2):
                comb = selg[g].T
                hi = comb.astype(BF16)
                comb_hi[g] = hi
                comb_lo[g] = (comb - hi.astype(F32)).astype(BF16)
        for g in range(2):
            back.wait(*hpiece(g, p))
        total = jnp.zeros((toks, 2 * w), F32)
        for g in range(2):
            got = wide([ret[h, g, :, a:a + w] for h in range(2)])
            total += dot(comb_hi[g], got) + dot(comb_lo[g], got)
        for h in range(2):
            tsend[h, :, a:a + w] = total[:, h * w:(h + 1) * w].astype(BF16)
        tcopy(p).start()

    def weigh(_, p):
        a, w = rspans[p]
        tcopy(p).wait_recv()
        tangents = []
        for h in range(2):
            total = tsend[h, :, a:a + w].astype(F32) + trecv[h, :, a:a + w].astype(F32)
            tangents.append(total.astype(BF16))
        for g in range(2):
            rows = (dot(sel[g], wide(tangents)) * gsl[g]).astype(BF16)
            for h in range(2):
                wsend[at.b, h, g, :, a:a + w] = rows[:, h * w:(h + 1) * w]
        out_w.start(*wpiece(p))
        tan_ref[:, a:a + w] = jnp.where(at.h == 0, tangents[0], tangents[1])
        for h in range(2):
            for g in range(2):
                wbuf[at.c, at.b, h, g, mine, a:a + w] = wsend[at.b, h, g, mine, a:a + w]

    def pcopy(kind, p):
        a, w = rspans[p]
        if kind == 0:
            ref = wbuf.at[at.c, at.b, :, :, :, pl.ds(a, w)]
        else:
            ref = wbuf.at[at.c, 1 - at.b, at.chip(3 if kind == 1 else 1) // 2, :, :, pl.ds(a, w)]
        return pltpu.make_async_remote_copy(
            src_ref=ref, dst_ref=ref, send_sem=p_sem.at[0, p, kind],
            recv_sem=p_sem.at[1, p, kind], device_id=at.pair(), device_id_type=MESH)

    def w_one(_, p):
        out_w.wait(*wpiece(p))
        out_v.start(*vpiece(p))
        pcopy(0, p).start()

    def w_two(_, p):
        for kind in range(2):
            out_v.copy(kind, *vpiece(p)).wait_recv()
            pcopy(1 + kind, p).start()

    def product(_, p):
        a, w = rspans[p]
        if p == 0:
            for g in range(2):
                hid_t[g] = hid[g, :, own].astype(F32).T.astype(BF16)
        for kind in range(3):
            pcopy(kind, p).wait_recv()
        for k in range(0, 8, 2):
            c, b, h = cbh(k)
            v = sum(dot(hid_t[g], wide([wbuf[c, b, h, g, :, a:a + w] for c in range(2)]))
                    for g in range(2))
            for c in range(2):
                gn_ref[0, :, (k + c) * chunk + a:(k + c) * chunk + a + w] = v[:, c * w:(c + 1) * w]

    for copy in loads[2:]:
        copy.wait()
    pl.semaphore_wait(barrier, experts - 1 + 4)
    steps = {
        "a": choose, "1": d_one, "u": up, "e": exchange, "s": silu, "n": near,
        "h": home, "c": combine, "w": weigh, "3": w_one, "4": w_two, "p": product}
    order = plan(dwidths, rwidths, direct, *options)[0]
    first_up = [step for step in order if step[0] == "u"][0][1:]
    up_seen = [0, 0]
    for count, (kind, g, p) in enumerate(order):
        steps[kind](g, p)
        if count == 0:
            for k in (0, 1, 2):
                for x in range(4):
                    shared[3 * x + k].start()

    for copy in shared:
        copy.wait_send()
    for g in range(2):
        ecopy(g).wait_send()
        for p in range(nd):
            out_a.drain(*apiece(g, p))
            if (g, p) not in direct:
                out_g.drain(*xpiece(g, p))
    for p in range(nr):
        for g in range(2):
            back.drain(*hpiece(g, p))
            for kind in range(2):
                rcopy(kind, g, p).wait_send()
        tcopy(p).wait_send()
        out_w.drain(*wpiece(p))
        out_v.drain(*vpiece(p))
        for kind in range(3):
            pcopy(kind, p).wait_send()


def on_device(
    dwidths, rwidths, direct, cap, options, tokens, w_gate, w_up, tangent_down, gates, expert_ids
):
    experts = lax.axis_size("ep")
    toks, width = tokens.shape
    topk = gates.shape[1]
    chunk = width // 8
    hidden = w_gate.shape[2]
    half = experts * cap
    nd, nr = len(dwidths), len(rwidths)
    vmem, anywhere = pl.BlockSpec(memory_space=pltpu.VMEM), pl.BlockSpec(memory_space=pl.ANY)
    return pl.pallas_call(
        functools.partial(kernel, dwidths, rwidths, direct, experts, cap, options),
        out_shape=(
            pltpu.VMEM((1, hidden, width), F32),
            pltpu.VMEM((toks, chunk), BF16),
        ),
        in_specs=[anywhere] * 6,
        out_specs=(vmem, vmem),
        scratch_shapes=[
            pltpu.VMEM((topk, toks), jnp.int32),
            pltpu.VMEM((topk, toks), F32),
            pltpu.VMEM((2, 2, toks, chunk), BF16),
            pltpu.VMEM((4, chunk, 2 * hidden), BF16),
            pltpu.VMEM((4, chunk, 2 * hidden), BF16),
            pltpu.VMEM((4, 2 * hidden, chunk), BF16),
            pltpu.VMEM((2, half, toks), BF16),
            pltpu.VMEM((2, half, toks), F32),
            pltpu.VMEM((2, half, 1), F32),
            pltpu.VMEM((2, toks, half), BF16),
            pltpu.VMEM((2, toks, half), BF16),
            pltpu.VMEM((2, 2, 2, half, chunk), BF16),
            pltpu.VMEM((2, 2, 2, half, chunk), BF16),
            pltpu.VMEM((2, half, 4 * hidden), F32),
            pltpu.VMEM((2, half, 4 * hidden), F32),
            pltpu.VMEM((2, half, 2 * hidden), BF16),
            pltpu.VMEM((2, hidden, half), BF16),
            pltpu.VMEM((2, 2, half, chunk), BF16),
            pltpu.VMEM((2, 2, half, chunk), BF16),
            pltpu.VMEM((2, 2, half, chunk), BF16),
            pltpu.VMEM((2, 2, half, chunk), BF16),
            pltpu.VMEM((2, toks, chunk), BF16),
            pltpu.VMEM((2, toks, chunk), BF16),
            pltpu.VMEM((2, 2, 2, half, chunk), BF16),
            pltpu.VMEM((2, 2, 2, 2, half, chunk), BF16),
            pltpu.SemaphoreType.DMA((18,)),
            pltpu.SemaphoreType.DMA((2, 12)),
            pltpu.SemaphoreType.DMA((2, 2 * nd)),
            pltpu.SemaphoreType.DMA((2, 2 * nr)),
            pltpu.SemaphoreType.DMA((2, nr)),
            pltpu.SemaphoreType.DMA((2 * nd, 2)),
            pltpu.SemaphoreType.DMA((2 * nd, 2)),
            pltpu.SemaphoreType.DMA((nr, 2)),
            pltpu.SemaphoreType.DMA((nr, 2)),
            pltpu.SemaphoreType.DMA((2, nr, 3)),
            pltpu.SemaphoreType.DMA((2, 2)),
            pltpu.SemaphoreType.DMA((2 * nr, 2)),
            pltpu.SemaphoreType.DMA((2 * nr, 2)),
            pltpu.SemaphoreType.DMA((2, nr)),
        ],
        compiler_params=pltpu.CompilerParams(
            collective_id=0, has_side_effects=True, vmem_limit_bytes=50 * 2**20),
    )(expert_ids.T, gates.T, tokens, w_gate, w_up, tangent_down)


def solution(
    mesh, dwidths=(128,) * 7, rwidths=(128,) * 7, direct=((1, 6),), cap=16, options=()
):
    in_specs = (
        P("ep", None),
        P("ep", None, "fsdp"),
        P("ep", None, "fsdp"),
        P("ep", "fsdp", None),
        P("ep", None),
        P("ep", None),
    )
    out_specs = (P("ep", "fsdp", None), P("ep", "fsdp"))
    return jax.shard_map(
        functools.partial(on_device, dwidths, rwidths, direct, cap, options),
        mesh=mesh, in_specs=in_specs, out_specs=out_specs, check_vma=False,
    )
```

time: 102 us -> 95.2 us (0.933)
  Pallas kernels: 97.1 us -> 90.7 us
    pallas_call x1, Pallas kernels: 97.1 us -> 90.7 us  [on_device(): pl.pallas_call(functools.partial(kernel, dwidths, rwidths, direct, expert...]
where the time goes in v4:
time: 95.2 us; the launch traced here: 95.1 us
  Pallas kernels  90.7 us (95%)
  local copies, waits for them, and re-layouts  3.74 us (4%)
    pallas_call x1, Pallas kernels, on_device(): pl.pallas_call(functools.partial(kernel, dwidths, rwidths, direct, expert...  90.7 us
    unnamed x2, local copies, waits for them, and re-layouts  3.74 us

profile of v4, /device:TPU:1, one launch (start us, length us, event | category | flops | bytes accessed | tf_op | source)
XLA Modules:
  0.0 95.1 jit_solution(14838166429295493811)
XLA Ops:
  0.6 90.7 %shard_map.77 = (f32[1,256,7168]{2,1,0:T(8,128)S(1)}, bf16[128,896]{1,0:T(8,128)(2,1)S(1)}) custom-call(s32[2,128]{1,0:T(2,128)} %bitcast.2, f32[2,128]{1,0:T(2,128)} %bitcast.3, bf16[128,7168]{1,0:T(8,128)(2,1)} %tok_ref.1, bf16[1,7168,256]{2,1,0:T(8,128)(2,1)} %wg_ref.1, bf16[1,7168,256]{2,1,0:T(8,128)(2,1)} %wu_ref.1, bf16[1,256,7168]{2,1,0:T(8,128)(2,1)} %td_ref.1), custom_call_target="tpu_custom_call" | custom-call | tf_op jit(solution)/shard_map/pallas_call | solution.py:486
  91.3 3.1 %copy.10 = f32[1,256,7168]{2,1,0:T(8,128)} copy(f32[1,256,7168]{2,1,0:T(8,128)S(1)} %get-tuple-element.2) | data formatting | bytes 14680064
  94.4 0.7 copy.11

commit v5 on v4

--- a/solution.py
+++ b/solution.py
@@ -117,7 +117,7 @@
             self.copy(kind, *piece).wait_send()
 
 
-def plan(dwidths, rwidths, direct, delay=(3.0, 4.0, 2.5)):
+def plan(dwidths, rwidths, direct, wdirect, delay=(3.0, 4.0, 2.5)):
     nd, nr = len(dwidths), len(rwidths)
     wd, wr = [w / 896 for w in dwidths], [w / 896 for w in rwidths]
     delay = dict(zip(("x", "yz", "pair"), delay))
@@ -141,9 +141,15 @@
     for p in range(nr):
         w, i = wr[p], 40 + p
         steps["c", 0, p] = (i, 1.4 * w, [("h", 0, p), ("h", 1, p)], [("x", 10 * w)])
-        steps["w", 0, p] = (i, 0.4 + 1.6 * w, [("c", 0, p)], [("yz", 20 * w)])
-        steps["3", 0, p] = (i, 0.1, [("w", 0, p)], [("x", 20 * w), ("pair", 4 * w)])
-        steps["4", 0, p] = (i, 0.1, [("3", 0, p)], [("pair", 4 * w)])
+        if p in wdirect:
+            steps["w", 0, p] = (i, 0.4 + 1.6 * w, [("c", 0, p)], [("x", 5 * w), ("yz", 20 * w)])
+            steps["v", 0, p] = (i, 0.4 + 1.6 * w, [("x", 0, p)], [("yz", 20 * w)])
+            steps["3", 0, p] = (i, 0.1, [("w", 0, p)], [("pair", 4 * w)])
+            steps["4", 0, p] = (i, 0.1, [("3", 0, p), ("v", 0, p)], [("pair", 4 * w)])
+        else:
+            steps["w", 0, p] = (i, 0.4 + 1.6 * w, [("c", 0, p)], [("yz", 20 * w)])
+            steps["3", 0, p] = (i, 0.1, [("w", 0, p)], [("x", 20 * w), ("pair", 4 * w)])
+            steps["4", 0, p] = (i, 0.1, [("3", 0, p)], [("pair", 4 * w)])
         steps["p", 0, p] = (200 + i, 2.4 * w, [("4", 0, p)], [])
     now, free, order = 0.0, {"x": 0.0, "yz": 0.0, "pair": 0.0}, []
     there = {"weights": 11.0}
@@ -160,18 +166,20 @@
         for link, time in steps[step][3]:
             free[link] = max(free[link], now) + time
             there[step] = max(there[step], free[link] + delay[link])
+            if step[0] == "w" and link == "x":
+                there["x", 0, step[2]] = there[step]
         order.append(step)
     return order, now
 
 
 def kernel(
-    dwidths, rwidths, direct, experts, cap, options,
+    dwidths, rwidths, direct, wdirect, experts, cap, options,
     ids_hbm, gates_hbm, tok_ref, wg_ref, wu_ref, td_ref,
     gn_ref, tan_ref,
     ids_ref, gates_ref, tokv, wgv, wuv, tdv, sel, selg, gsl, comb_hi, comb_lo, send, xbuf, acc,
-    acc_in, hid, hid_t, rsend, rrecv, fin, ret, tsend, trecv, wsend, wbuf,
+    acc_in, hid, hid_t, rsend, rrecv, fin, ret, tsend, trecv, tang, wsend, wbuf,
     load, v_sem, x_sem, h_sem, w_sem, xg_send, xg_recv, g_send, g_recv, p_sem, e_sem, r_send,
-    r_recv, t_sem,
+    r_recv, t_sem, u_sem, w2_sem,
 ):
     at = Place()
     dspans, rspans = spans(dwidths), spans(rwidths)
@@ -247,6 +255,7 @@
     out_g = Gather(at, xbuf, xg_send, xg_recv)
     back = AllToAll(at, experts, cap, fin, ret, h_sem)
     out_w = AllToAll(at, experts, cap, wsend, wbuf.at[at.c], w_sem)
+    out_w2 = AllToAll(at, experts, cap, wsend, wbuf.at[at.c], w2_sem)
     out_v = Gather(at, wbuf.at[at.c], g_send, g_recv)
 
     def apiece(g, p):
@@ -261,6 +270,9 @@
 
     def wpiece(p):
         return p, (at.b, both, both), *rspans[p]
+
+    def w2piece(p):
+        return p, (1 - at.b, both, both), *rspans[p]
 
     def vpiece(p):
         return p, both, *rspans[p]
@@ -385,6 +397,25 @@
             tsend[h, :, a:a + w] = total[:, h * w:(h + 1) * w].astype(BF16)
         tcopy(p).start()
 
+    def ucopy(kind, p):
+        a, w = rspans[p]
+        ref = tang.at[at.b, at.h, :, pl.ds(a, w)]
+        return pltpu.make_async_remote_copy(
+            src_ref=ref, dst_ref=ref, send_sem=u_sem.at[0, p, kind],
+            recv_sem=u_sem.at[1, p, kind], device_id=at.to(1 if kind == 0 else 3),
+            device_id_type=MESH)
+
+    def scale(p, b, tangents, send):
+        a, w = rspans[p]
+        for g in range(2):
+            rows = (dot(sel[g], wide(tangents)) * gsl[g]).astype(BF16)
+            for h in range(2):
+                wsend[b, h, g, :, a:a + w] = rows[:, h * w:(h + 1) * w]
+        send()
+        for h in range(2):
+            for g in range(2):
+                wbuf[at.c, b, h, g, mine, a:a + w] = wsend[b, h, g, mine, a:a + w]
+
     def weigh(_, p):
         a, w = rspans[p]
         tcopy(p).wait_recv()
@@ -392,15 +423,20 @@
         for h in range(2):
             total = tsend[h, :, a:a + w].astype(F32) + trecv[h, :, a:a + w].astype(F32)
             tangents.append(total.astype(BF16))
-        for g in range(2):
-            rows = (dot(sel[g], wide(tangents)) * gsl[g]).astype(BF16)
-            for h in range(2):
-                wsend[at.b, h, g, :, a:a + w] = rows[:, h * w:(h + 1) * w]
-        out_w.start(*wpiece(p))
+            if p in wdirect:
+                tang[at.b, h, :, a:a + w] = tangents[h]
+        if p in wdirect:
+            for kind in range(2):
+                ucopy(kind, p).start()
+        scale(p, at.b, tangents, lambda: out_w.start(*wpiece(p)))
         tan_ref[:, a:a + w] = jnp.where(at.h == 0, tangents[0], tangents[1])
-        for h in range(2):
-            for g in range(2):
-                wbuf[at.c, at.b, h, g, mine, a:a + w] = wsend[at.b, h, g, mine, a:a + w]
+
+    def others(_, p):
+        a, w = rspans[p]
+        for kind in range(2):
+            ucopy(kind, p).wait_recv()
+        scale(p, 1 - at.b, [tang[1 - at.b, h, :, a:a + w] for h in range(2)],
+              lambda: out_w2.start(*w2piece(p)))
 
     def pcopy(kind, p):
         a, w = rspans[p]
@@ -414,12 +450,16 @@
 
     def w_one(_, p):
         out_w.wait(*wpiece(p))
-        out_v.start(*vpiece(p))
+        if p not in wdirect:
+            out_v.start(*vpiece(p))
         pcopy(0, p).start()
 
     def w_two(_, p):
+        if p in wdirect:
+            out_w2.wait(*w2piece(p))
         for kind in range(2):
-            out_v.copy(kind, *vpiece(p)).wait_recv()
+            if p not in wdirect:
+                out_v.copy(kind, *vpiece(p)).wait_recv()
             pcopy(1 + kind, p).start()
 
     def product(_, p):
@@ -441,8 +481,8 @@
     pl.semaphore_wait(barrier, experts - 1 + 4)
     steps = {
         "a": choose, "1": d_one, "u": up, "e": exchange, "s": silu, "n": near,
-        "h": home, "c": combine, "w": weigh, "3": w_one, "4": w_two, "p": product}
-    order = plan(dwidths, rwidths, direct, *options)[0]
+        "h": home, "c": combine, "w": weigh, "v": others, "3": w_one, "4": w_two, "p": product}
+    order = plan(dwidths, rwidths, direct, wdirect, *options)[0]
     first_up = [step for step in order if step[0] == "u"][0][1:]
     up_seen = [0, 0]
     for count, (kind, g, p) in enumerate(order):
@@ -467,13 +507,34 @@
                 rcopy(kind, g, p).wait_send()
         tcopy(p).wait_send()
         out_w.drain(*wpiece(p))
-        out_v.drain(*vpiece(p))
+        if p in wdirect:
+            out_w2.drain(*w2piece(p))
+            for kind in range(2):
+                ucopy(kind, p).wait_send()
+        else:
+            out_v.drain(*vpiece(p))
         for kind in range(3):
             pcopy(kind, p).wait_send()
 
 
+PARTS = 8
+
+
+def store(gn_ref, tan_ref, gn_out, tan_out, sems):
+    rows = gn_ref.shape[1] // PARTS
+    copies = [pltpu.make_async_copy(
+        gn_ref.at[:, pl.ds(k * rows, rows), :], gn_out.at[:, pl.ds(k * rows, rows), :], sems.at[k])
+        for k in range(PARTS)]
+    copies.append(pltpu.make_async_copy(tan_ref, tan_out, sems.at[PARTS]))
+    for copy in copies:
+        copy.start()
+    for copy in copies:
+        copy.wait()
+
+
 def on_device(
-    dwidths, rwidths, direct, cap, options, tokens, w_gate, w_up, tangent_down, gates, expert_ids
+    dwidths, rwidths, direct, wdirect, cap, options,
+    tokens, w_gate, w_up, tangent_down, gates, expert_ids,
 ):
     experts = lax.axis_size("ep")
     toks, width = tokens.shape
@@ -483,8 +544,8 @@
     half = experts * cap
     nd, nr = len(dwidths), len(rwidths)
     vmem, anywhere = pl.BlockSpec(memory_space=pltpu.VMEM), pl.BlockSpec(memory_space=pl.ANY)
-    return pl.pallas_call(
-        functools.partial(kernel, dwidths, rwidths, direct, experts, cap, options),
+    gn, tangent = pl.pallas_call(
+        functools.partial(kernel, dwidths, rwidths, direct, wdirect, experts, cap, options),
         out_shape=(
             pltpu.VMEM((1, hidden, width), F32),
             pltpu.VMEM((toks, chunk), BF16),
@@ -515,6 +576,7 @@
             pltpu.VMEM((2, 2, half, chunk), BF16),
             pltpu.VMEM((2, toks, chunk), BF16),
             pltpu.VMEM((2, toks, chunk), BF16),
+            pltpu.VMEM((2, 2, toks, chunk), BF16),
             pltpu.VMEM((2, 2, 2, half, chunk), BF16),
             pltpu.VMEM((2, 2, 2, 2, half, chunk), BF16),
             pltpu.SemaphoreType.DMA((18,)),
@@ -531,14 +593,27 @@
             pltpu.SemaphoreType.DMA((2 * nr, 2)),
             pltpu.SemaphoreType.DMA((2 * nr, 2)),
             pltpu.SemaphoreType.DMA((2, nr)),
+            pltpu.SemaphoreType.DMA((2, nr, 2)),
+            pltpu.SemaphoreType.DMA((2, nr)),
         ],
         compiler_params=pltpu.CompilerParams(
             collective_id=0, has_side_effects=True, vmem_limit_bytes=50 * 2**20),
     )(expert_ids.T, gates.T, tokens, w_gate, w_up, tangent_down)
+    shapes = (
+        jax.ShapeDtypeStruct((1, hidden, width), F32), jax.ShapeDtypeStruct((toks, chunk), BF16))
+    return pl.pallas_call(
+        store,
+        out_shape=shapes,
+        in_specs=[vmem, vmem],
+        out_specs=(anywhere, anywhere),
+        scratch_shapes=[pltpu.SemaphoreType.DMA((PARTS + 1,))],
+        compiler_params=pltpu.CompilerParams(vmem_limit_bytes=2**20),
+    )(*[pltpu.with_memory_space_constraint(v, pltpu.VMEM) for v in (gn, tangent)])
 
 
 def solution(
-    mesh, dwidths=(128,) * 7, rwidths=(128,) * 7, direct=((1, 6),), cap=16, options=()
+    mesh, dwidths=(128,) * 7, rwidths=(128,) * 7, direct=((1, 6),), wdirect=(6,), cap=16,
+    options=(),
 ):
     in_specs = (
         P("ep", None),
@@ -550,6 +625,6 @@
     )
     out_specs = (P("ep", "fsdp", None), P("ep", "fsdp"))
     return jax.shard_map(
-        functools.partial(on_device, dwidths, rwidths, direct, cap, options),
+        functools.partial(on_device, dwidths, rwidths, direct, wdirect, cap, options),
         mesh=mesh, in_specs=in_specs, out_specs=out_specs, check_vma=False,
     )

time: 95.2 us -> 93.3 us (0.980)
  local copies, waits for them, and re-layouts: 3.74 us -> 0 us
  Pallas kernels: 90.7 us -> 92.4 us
    unnamed x2 -> x0, local copies, waits for them, and re-layouts: 3.74 us -> none
    pallas_call x1 -> x2, Pallas kernels: 90.7 us -> 92.4 us  [the longest x1 89.2 us: on_device(): pl.pallas_call(functools.partial(kernel, dwidths, rwidths, direct, wdirec...]
where the time goes in v5:
time: 93.3 us; the launch traced here: 93.2 us
  Pallas kernels  92.4 us (99%)
    pallas_call x1, Pallas kernels, on_device(): pl.pallas_call(functools.partial(kernel, dwidths, rwidths, direct, wdirec...  89.2 us
    pallas_call x1, Pallas kernels, on_device(): pl.pallas_call(store, out_shape=shapes, in_specs=[vmem, vmem], out_specs=...  3.11 us

profile of v5, /device:TPU:1, one launch (start us, length us, event | category | flops | bytes accessed | tf_op | source)
XLA Modules:
  0.0 93.2 jit_solution(10812130270580418163)
XLA Ops:
  0.6 89.2 %shard_map.77 = (f32[1,256,7168]{2,1,0:T(8,128)S(1)}, bf16[128,896]{1,0:T(8,128)(2,1)S(1)}) custom-call(s32[2,128]{1,0:T(2,128)} %bitcast.2, f32[2,128]{1,0:T(2,128)} %bitcast.3, bf16[128,7168]{1,0:T(8,128)(2,1)} %tok_ref.1, bf16[1,7168,256]{2,1,0:T(8,128)(2,1)} %wg_ref.1, bf16[1,7168,256]{2,1,0:T(8,128)(2,1)} %wu_ref.1, bf16[1,256,7168]{2,1,0:T(8,128)(2,1)} %td_ref.1), custom_call_target="tpu_custom_call" | custom-call | tf_op jit(solution)/shard_map/pallas_call | solution.py:547
  89.9 3.1 %shard_map.78 = (f32[1,256,7168]{2,1,0:T(8,128)}, bf16[128,896]{1,0:T(8,128)(2,1)}) custom-call(f32[1,256,7168]{2,1,0:T(8,128)S(1)} %get-tuple-element.4.gn_ref, bf16[128,896]{1,0:T(8,128)(2,1)S(1)} %get-tuple-element.5.tan_ref), custom_call_target="tpu_custom_call" | custom-call | tf_op jit(solution)/shard_map/pallas_call | solution.py:604

commit v6 on v5

--- a/solution.py
+++ b/solution.py
@@ -133,7 +133,7 @@
                 steps["1", g, p] = (i, 0.1, [("a", g, p)], [("x", 10 * w)])
                 steps["u", g, p] = (90 + i, 2.4 * w, [("1", g, p), "weights"], [])
         steps["e", g, 0] = (99, 0.1, [("u", g, p) for p in range(nd)], [("pair", 2.0)])
-        steps["s", g, 0] = (100, 1.0, [("e", g, 0)], [])
+        steps["s", g, 0] = (100, 0.6, [("e", g, 0)], [])
         for p in range(nr):
             w, i = wr[p], 20 + g * nr + p
             steps["n", g, p] = (i, 1.2 * w, [("s", g, 0)], [("x", 10 * w)])
@@ -278,16 +278,23 @@
         return p, both, *rspans[p]
 
     def choose(g, p):
+        if (g, p) != order[0][1:]:
+            prepare(g, p)
+        out_a.start(*apiece(g, p))
+        keep(g, p)
+
+    def which(g, p):
+        return chips if (g, p) in direct else [(at.b, h) for h in range(2)]
+
+    def prepare(g, p):
         a, w = dspans[p]
-        if (g, p) in direct:
-            which = [(b, h) for b, h in chips]
-        else:
-            which = [(at.b, h) for h in range(2)]
-        rows = dot(sel[g], wide([tokv[b, h, :, a:a + w] for b, h in which])).astype(BF16)
-        for k, (b, h) in enumerate(which):
+        rows = dot(sel[g], wide([tokv[b, h, :, a:a + w] for b, h in which(g, p)])).astype(BF16)
+        for k, (b, h) in enumerate(which(g, p)):
             send[b, h, g, :, a:a + w] = rows[:, k * w:(k + 1) * w]
-        out_a.start(*apiece(g, p))
-        for b, h in which:
+
+    def keep(g, p):
+        a, w = dspans[p]
+        for b, h in which(g, p):
             xbuf[b, h, g, mine, a:a + w] = send[b, h, g, mine, a:a + w]
 
     def d_one(g, p):
@@ -316,25 +323,34 @@
             acc[g, :, cols] = total
         up_seen[g] += 1
 
-    def ecopy(g):
+    def ecopy(g, m):
+        ref, there = (v.at[g, pl.ds(m * half // 2, half // 2), :] for v in (acc, acc_in))
         return pltpu.make_async_remote_copy(
-            src_ref=acc.at[g], dst_ref=acc_in.at[g], send_sem=e_sem.at[0, g],
-            recv_sem=e_sem.at[1, g], device_id=at.pair(), device_id_type=MESH)
+            src_ref=ref, dst_ref=there, send_sem=e_sem.at[0, g, m],
+            recv_sem=e_sem.at[1, g, m], device_id=at.pair(), device_id_type=MESH)
 
     def exchange(g, _):
-        ecopy(g).start()
+        for m in range(2):
+            ecopy(g, m).start()
+        comb = selg[g].T
+        hi = comb.astype(BF16)
+        comb_hi[g] = hi
+        comb_lo[g] = (comb - hi.astype(F32)).astype(BF16)
 
     def silu(g, _):
-        ecopy(g).wait_recv()
+        size = 2 * cap if half % (4 * cap) == 0 else cap
+        steps = half // 2 // size
 
         def tile(m, carry):
-            r = pl.ds(pl.multiple_of(m * cap, cap), cap)
+            r = pl.ds(pl.multiple_of(m * size, size), size)
             v = acc[g, r, :] + acc_in[g, r, :]
             gate, value = v[:, :2 * hidden], v[:, 2 * hidden:]
             hid[g, r, :] = (gate / (1.0 + jnp.exp(-gate)) * value).astype(BF16)
             return carry
 
-        lax.fori_loop(0, half // cap, tile, 0)
+        for m in range(2):
+            ecopy(g, m).wait_recv()
+            lax.fori_loop(m * steps, (m + 1) * steps, tile, 0)
         if g == 0:
             for x in range(4):
                 local[3 * x + 2].wait()
@@ -381,12 +397,6 @@
 
     def combine(_, p):
         a, w = rspans[p]
-        if p == 0:
-            for g in range(2):
-                comb = selg[g].T
-                hi = comb.astype(BF16)
-                comb_hi[g] = hi
-                comb_lo[g] = (comb - hi.astype(F32)).astype(BF16)
         for g in range(2):
             back.wait(*hpiece(g, p))
         total = jnp.zeros((toks, 2 * w), F32)
@@ -476,13 +486,14 @@
             for c in range(2):
                 gn_ref[0, :, (k + c) * chunk + a:(k + c) * chunk + a + w] = v[:, c * w:(c + 1) * w]
 
+    order = plan(dwidths, rwidths, direct, wdirect, *options)[0]
     for copy in loads[2:]:
         copy.wait()
+    prepare(*order[0][1:])
     pl.semaphore_wait(barrier, experts - 1 + 4)
     steps = {
         "a": choose, "1": d_one, "u": up, "e": exchange, "s": silu, "n": near,
         "h": home, "c": combine, "w": weigh, "v": others, "3": w_one, "4": w_two, "p": product}
-    order = plan(dwidths, rwidths, direct, wdirect, *options)[0]
     first_up = [step for step in order if step[0] == "u"][0][1:]
     up_seen = [0, 0]
     for count, (kind, g, p) in enumerate(order):
@@ -495,7 +506,8 @@
     for copy in shared:
         copy.wait_send()
     for g in range(2):
-        ecopy(g).wait_send()
+        for m in range(2):
+            ecopy(g, m).wait_send()
         for p in range(nd):
             out_a.drain(*apiece(g, p))
             if (g, p) not in direct:
@@ -589,7 +601,7 @@
             pltpu.SemaphoreType.DMA((nr, 2)),
             pltpu.SemaphoreType.DMA((nr, 2)),
             pltpu.SemaphoreType.DMA((2, nr, 3)),
-            pltpu.SemaphoreType.DMA((2, 2)),
+            pltpu.SemaphoreType.DMA((2, 2, 2)),
             pltpu.SemaphoreType.DMA((2 * nr, 2)),
             pltpu.SemaphoreType.DMA((2 * nr, 2)),
             pltpu.SemaphoreType.DMA((2, nr)),
@@ -612,7 +624,7 @@
 
 
 def solution(
-    mesh, dwidths=(128,) * 7, rwidths=(128,) * 7, direct=((1, 6),), wdirect=(6,), cap=16,
+    mesh, dwidths=(128,) * 7, rwidths=(128,) * 7, direct=((1, 4), (1, 5), (1, 6)), wdirect=(6,), cap=16,
     options=(),
 ):
     in_specs = (

time: 93.3 us -> 92.3 us (0.989)
  Pallas kernels: 92.4 us -> 91.4 us
    pallas_call x1, Pallas kernels: 89.2 us -> 88.3 us  [on_device(): pl.pallas_call(functools.partial(kernel, dwidths, rwidths, direct, wdirec...]
where the time goes in v6:
time: 92.3 us; the launch traced here: 92.2 us
  Pallas kernels  91.4 us (99%)
    pallas_call x1, Pallas kernels, on_device(): pl.pallas_call(functools.partial(kernel, dwidths, rwidths, direct, wdirec...  88.3 us
    pallas_call x1, Pallas kernels, on_device(): pl.pallas_call(store, out_shape=shapes, in_specs=[vmem, vmem], out_specs=...  3.11 us

profile of v6, /device:TPU:1, one launch (start us, length us, event | category | flops | bytes accessed | tf_op | source)
XLA Modules:
  0.0 92.2 jit_solution(3465955865180620410)
XLA Ops:
  0.6 88.3 %shard_map.77 = (f32[1,256,7168]{2,1,0:T(8,128)S(1)}, bf16[128,896]{1,0:T(8,128)(2,1)S(1)}) custom-call(s32[2,128]{1,0:T(2,128)} %bitcast.2, f32[2,128]{1,0:T(2,128)} %bitcast.3, bf16[128,7168]{1,0:T(8,128)(2,1)} %tok_ref.1, bf16[1,7168,256]{2,1,0:T(8,128)(2,1)} %wg_ref.1, bf16[1,7168,256]{2,1,0:T(8,128)(2,1)} %wu_ref.1, bf16[1,256,7168]{2,1,0:T(8,128)(2,1)} %td_ref.1), custom_call_target="tpu_custom_call" | custom-call | tf_op jit(solution)/shard_map/pallas_call | solution.py:559
  88.9 3.1 %shard_map.78 = (f32[1,256,7168]{2,1,0:T(8,128)}, bf16[128,896]{1,0:T(8,128)(2,1)}) custom-call(f32[1,256,7168]{2,1,0:T(8,128)S(1)} %get-tuple-element.4.gn_ref, bf16[128,896]{1,0:T(8,128)(2,1)S(1)} %get-tuple-element.5.tan_ref), custom_call_target="tpu_custom_call" | custom-call | tf_op jit(solution)/shard_map/pallas_call | solution.py:616
